TPU v7x, 32 devices: a whole 2x2x4 slice. The times are simulated.
32 devices in a mesh: ctx: 2 (over x), ch: 16 (over z, y, core).
Axes of the slice: x: 2, y: 2, z: 4, core: 2. Of those that a mesh axis runs over, the one named last changes fastest.
Arguments:
- first_in: bfloat16 [512, 16384], P('ch', 'ctx'), may hold values from -6 to 6
- second_in: bfloat16 [512, 16384], P('ch', 'ctx'), may hold values from -6 to 6
- third_in: bfloat16 [512, 16384], P('ch', 'ctx'), may hold values from -6 to 6
- grad_heads: bfloat16 [512, 16384], P(None, ('ctx', 'ch')), may hold values from -6 to 6
- residue: float32 [32, 16], P('ch'), may hold values from -1.5 to 1.5
- decay_rate: float32 [32, 16], P('ch'), may hold values from 1.2207031e-05 to 0.1, as said below
- skip_gain: float32 [512], P('ch'), may hold values from -3 to 3
Outputs:
- grad_first: bfloat16 [512, 16384], P('ch', 'ctx')
- grad_second: bfloat16 [512, 16384], P('ch', 'ctx')
- grad_third: bfloat16 [512, 16384], P('ch', 'ctx')
- grad_residue: float32 [32, 16], P('ch')
- grad_skip: float32 [512], P('ch')
Inputs may be any that keep to these rules, and one draw needn't show every extreme that they name: `decay_rate`: positive decay rate of each mode.
All inputs are finite; a program needn't handle non-finite values.
Results may differ from a plain program's by a relative error of at most 0.006.
Values may be sent and summed in bfloat16 or wider, within the bound.
A program may use at most 64 MiB of HBM per device.

v0:
```python
import jax
import jax.numpy as jnp
from jax import lax
from jax.sharding import PartitionSpec as P

PRECISE = lax.Precision.HIGHEST


def carried_in(array, axis, combine, identity, reverse):
    devices, place = (lax.axis_size(axis), lax.axis_index(axis))
    everything = jax.tree.map(lambda part: lax.all_gather(part, axis), array)
    start = jax.tree.map(
        lambda part, zero: jnp.broadcast_to(jnp.asarray(zero, part.dtype), part.shape),
        array,
        identity,
    )

    def step(k, before):
        at = devices - 1 - k if reverse else k
        reached = at > place if reverse else at < place
        new = combine(before, jax.tree.map(lambda part: part[at], everything))
        return jax.tree.map(lambda a, b: jnp.where(reached, a, b), new, before)

    return lax.fori_loop(0, devices, step, start)


def link_states(earlier, later):
    return (later[0] + later[1][:, None, :] * earlier[0], earlier[1] * later[1])


def on_device(first_in, second_in, third_in, grad_heads, residue, decay_rate, skip_gain):
    channels, length = first_in.shape
    groups, mode_count = residue.shape
    group_width = channels // groups
    block_len = min(512, length)
    span_count = length // block_len
    ctx_count = lax.axis_size("ctx")
    seq_total = length * ctx_count
    split_shape = (groups, group_width, span_count, block_len)
    mode_weight = residue * jnp.sqrt(2.0 * decay_rate)
    rate_col = decay_rate[:, :, None]
    rate_box = decay_rate[:, :, None, None] * block_len
    offsets = jnp.arange(block_len, dtype=jnp.float32)
    middle = offsets - float(block_len // 2)
    falling = jnp.exp(-rate_col * middle)
    rising = jnp.exp(rate_col * middle)
    lower_mask = offsets[:, None] >= offsets[None, :]
    toeplitz = jnp.einsum(
        "gri,grj->gij", mode_weight[:, :, None] * falling, rising, precision=PRECISE
    )
    toeplitz = jnp.where(lower_mask[None], toeplitz, 0.0)
    decay_in = jnp.exp(-rate_col * offsets)
    tail_decay = jnp.exp(-rate_col * (block_len - offsets))
    head_decay = jnp.exp(-rate_col * (offsets + 1.0))
    rise_modes = mode_weight[:, :, None] * decay_in
    fall_modes = mode_weight[:, :, None] * jnp.exp(-rate_col * (block_len - 1.0 - offsets))
    span_pos = jnp.arange(span_count, dtype=jnp.float32)
    later_decay = jnp.exp(-rate_col * block_len * (span_count - 1.0 - span_pos))
    start_decay = jnp.exp(-rate_col * block_len * span_pos)
    span_gap = span_pos[:, None] - 1.0 - span_pos[None, :]
    between = jnp.where(span_gap >= 0.0, jnp.exp(-rate_box * jnp.maximum(span_gap, 0.0)), 0.0)
    block_decay = jnp.exp(-decay_rate * length)
    skip_split = skip_gain.reshape(groups, group_width, 1, 1)
    gated = first_in.astype(jnp.float32) * second_in.astype(jnp.float32)
    gated_split = gated.reshape(split_shape)
    within = jnp.einsum("gcnj,gij->gcni", gated_split, toeplitz, precision=PRECISE)
    span_state = jnp.einsum("gcnj,grj->gcnr", gated_split, tail_decay, precision=PRECISE)
    fwd_local = jnp.einsum("gcnr,grn->gcr", span_state, later_decay, precision=PRECISE)
    grad_out = lax.all_to_all(grad_heads, "ch", split_axis=0, concat_axis=1, tiled=True)
    grad_conv = grad_out.astype(jnp.float32) * third_in.astype(jnp.float32)
    grad_split = grad_conv.reshape(split_shape)
    back_within = jnp.einsum("gcni,gij->gcnj", grad_split, toeplitz, precision=PRECISE)
    back_state = jnp.einsum("gcni,gri->gcnr", grad_split, head_decay, precision=PRECISE)
    bwd_local = jnp.einsum("gcnr,grn->gcr", back_state, start_decay, precision=PRECISE)
    identity = (jnp.zeros_like(fwd_local), jnp.ones_like(block_decay))
    enter_fwd = carried_in((fwd_local, block_decay), "ctx", link_states, identity, False)[0]
    enter_bwd = carried_in((bwd_local, block_decay), "ctx", link_states, identity, True)[0]
    enter_spans = jnp.einsum("grnm,gcmr->gcnr", between, span_state, precision=PRECISE)
    enter_spans = enter_spans + jnp.einsum(
        "grn,gcr->gcnr", start_decay, enter_fwd, precision=PRECISE
    )
    convolved = (
        within
        + jnp.einsum("gcnr,gri->gcni", enter_spans, rise_modes, precision=PRECISE)
        + skip_split * gated_split
    )
    grad_third = (grad_out.astype(jnp.float32) * convolved.reshape(channels, length)).astype(
        jnp.bfloat16
    )
    leave_spans = jnp.einsum("grmn,gcmr->gcnr", between, back_state, precision=PRECISE)
    leave_spans = leave_spans + jnp.einsum(
        "grn,gcr->gcnr", later_decay, enter_bwd, precision=PRECISE
    )
    grad_mixed = (
        back_within
        + jnp.einsum("gcnr,gri->gcni", leave_spans, fall_modes, precision=PRECISE)
        + skip_split * grad_split
    )
    grad_mixed = grad_mixed.reshape(channels, length)
    grad_first = (grad_mixed * second_in.astype(jnp.float32)).astype(jnp.bfloat16)
    grad_second = (grad_mixed * first_in.astype(jnp.float32)).astype(jnp.bfloat16)
    cross_sums = jnp.einsum("gcni,gcnj->gij", grad_split, gated_split, precision=PRECISE)
    cross_sums = jnp.where(lower_mask[None], cross_sums, 0.0)
    folded = jnp.einsum("gij,grj->gri", cross_sums, rising, precision=PRECISE)
    near_part = jnp.sum(folded * falling, axis=2)
    weighted = jnp.einsum("gcni,gri->gcnr", grad_split, decay_in, precision=PRECISE)
    far_part = jnp.sum(weighted * enter_spans, axis=(1, 2))
    filter_part = jnp.sqrt(2.0 * decay_rate) * (near_part + far_part)
    skip_part = jnp.sum(grad_conv * gated, axis=1)
    filter_sum, skip_sum = lax.psum((filter_part, skip_part), "ctx")
    grad_residue = filter_sum / jnp.sqrt(float(group_width * seq_total))
    grad_skip = skip_sum / jnp.sqrt(float(seq_total))
    return (grad_first, grad_second, grad_third, grad_residue, grad_skip)


def solution(mesh):
    return jax.shard_map(
        on_device,
        mesh=mesh,
        in_specs=(
            P("ch", "ctx"),
            P("ch", "ctx"),
            P("ch", "ctx"),
            P(None, ("ctx", "ch")),
            P("ch", None),
            P("ch", None),
            P("ch"),
        ),
        out_specs=(P("ch", "ctx"), P("ch", "ctx"), P("ch", "ctx"), P("ch", None), P("ch")),
        check_vma=False,
    )
```

profile of v0, /device:TPU:0, one launch (start us, length us, event | category | flops | bytes accessed | tf_op | source)
XLA Modules:
  0.0 64.1 jit_solution(718487531428816240)
XLA Ops:
  0.6 7.4 %all-to-all-start = ((bf16[16,32,512]{2,1,0:T(8,128)(2,1)}), bf16[16,32,512]{2,1,0:T(8,128)(2,1)}, u32[]{:S(2)}, u32[]{:S(2)}) async-start(bf16[16,32,512]{2,1,0:T(8,128)(2,1)} %bitcast.165), calls=%async_computation | async-start | bytes 1048576 | tf_op jit(solution)/shard_map/all_to_all | solution.py:69
  8.1 0.1 fusion.87
  8.2 0.1 fusion.88
  8.3 0.2 iota_compare_fusion
  8.5 0.7 %fusion.89 = (f32[2,16]{1,0:T(2,128)S(1)}, f32[2,16]{1,0:T(2,128)S(1)}, f32[1,2,16]{2,1,0:T(2,128)S(1)}, f32[2,16]{1,0:T(2,128)S(1)}, f32[2,16]{1,0:T(2,128)S(1)}) fusion(f32[2,16]{1,0:T(2,128)} %param.15, f32[2,16]{1,0:T(2,128)} %param.16), kind=kLoop, calls=%fused_computation.116 | loop fusion | flops 224 | bytes 896 | tf_op jit(solution)/shard_map/mul | solution.py:40
  9.2 0.1 multiply_exponential_fusion.9
  9.3 0.1 copy.51
  9.4 1.3 %convert_multiply_fusion = f32[32,8192]{1,0:T(8,128)S(1)} fusion(bf16[32,8192]{1,0:T(8,128)(2,1)} %param.11, bf16[32,8192]{1,0:T(8,128)(2,1)} %param.12), kind=kLoop, calls=%fused_computation.18 | loop fusion | flops 786432 | bytes 2097152 | tf_op jit(solution)/shard_map/mul | solution.py:64
  10.7 0.6 copy.57
  11.3 1.0 %multiply_reduce_fusion.1 = (f32[2,16,16]{1,2,0:T(8,128)S(1)}, f32[2,16,16,16]{3,2,1,0:T(8,128)S(1)}) fusion(f32[2,16,16]{1,2,0:T(8,128)S(1)} %copy.51, f32[512]{0:T(512)S(1)} %iota_subtract_fusion.1, f32[2,16]{1,0:T(2,128)S(1)} %get-tuple-element.299, f32[2,16,16,512]{3,2,1,0:T(8,128)S(1)} %bitcast.152), kind=kOutput, calls=%fused_computation.53 | convolution fusion | flops 50363904 | bytes 1087616 | tf_op jit(solution)/shard_map/gcnj,grj->gcnr/dot_general | solution.py:67
  12.4 4.4 %all-gather.2 = f32[4,16,16]{2,1,0:T(8,128)S(1)} all-gather(f32[2,16,16]{2,1,0:T(8,128)S(1)} %bitcast.169), channel_id=4, replica_groups=mesh['ctx'=2,'ch'=16] {'ctx'}, dimensions={0}, use_global_device_ids=true | all-gather | bytes 6144 | tf_op jit(solution)/shard_map/all_gather | solution.py:11
  16.8 4.4 %all-gather.3 = f32[2,2,16]{2,1,0:T(2,128)S(1)} all-gather(f32[1,2,16]{2,1,0:T(2,128)S(1)} %get-tuple-element.298), channel_id=3, replica_groups=mesh['ctx'=2,'ch'=16] {'ctx'}, dimensions={0}, use_global_device_ids=true | all-gather | bytes 384 | tf_op jit(solution)/shard_map/all_gather | solution.py:11
  21.2 0.1 while.37
  21.3 0.1 copy.28
  21.4 0.2 copy.27
  21.6 0.1 mul.280
  21.6 0.1 copy.50
  21.7 0.6 fusion.21
  22.3 1.0 %fusion.44 = f32[2,16,16,512]{3,2,1,0:T(8,128)S(1)} fusion(f32[2,16,16,16]{2,1,3,0:T(8,128)S(1)} %fusion.21, f32[2,16]{1,0:T(2,128)S(1)} %get-tuple-element.299, f32[2,16]{1,0:T(2,128)S(1)} %get-tuple-element.296), kind=kOutput, calls=%fused_computation.55 | convolution fusion | flops 50364416 | bytes 1081600 | tf_op jit(solution)/shard_map/gcnr,gri->gcni/dot_general | solution.py:84
  23.4 2.0 %fusion.69 = f32[2,512,512]{2,1,0:T(8,128)S(1)} fusion(f32[2,16]{1,0:T(2,128)S(1)} %copy-done.8, f32[512]{0:T(512)S(1)} %iota_add_fusion.1, f32[2,16]{1,0:T(2,128)S(1)} %get-tuple-element.299, f32[2,16]{1,0:T(2,128)S(1)} %get-tuple-element.296), kind=kOutput, calls=%fused_computation.84 | convolution fusion | flops 100712448 | bytes 2099584 | tf_op jit(solution)/shard_map/gri,grj->gij/dot_general | solution.py:48
  25.4 2.2 %fusion.18 = f32[2,16,16,512]{3,2,1,0:T(8,128)S(1)} fusion(f32[2,16,16,512]{3,2,1,0:T(8,128)S(1)} %fusion.44, f32[2,512,512]{2,1,0:T(8,128)S(1)} %fusion.69, pred[512,512]{1,0:T(8,128)(4,1)S(1)} %iota_compare_fusion, f32[2,16]{1,0:T(2,128)S(1)} %mul.280, f32[2,16,16,512]{3,2,1,0:T(8,128)S(1)} %bitcast.153, f32[2,16,16,512]{3,2,1,0:T(8,128)S(1)} %bitcast.154), kind=kOutput, calls=%fused_computation.17 | convolution fusion | flops 1611923456 | bytes 6553728 | tf_op jit(solution)/shard_map/gcnj,gij->gcni/dot_general | solution.py:66
  27.6 1.6 %copy.58 = f32[4,8,16,512]{3,1,2,0:T(8,128)} copy(f32[4,8,16,512]{3,2,1,0:T(8,128)S(1)} %bitcast.162) | data formatting | bytes 2097152
  29.3 1.3 %convert_bitcast_fusion = f32[16,4,8,512]{3,2,1,0:T(8,128)S(1)} fusion(bf16[16,32,512]{2,1,0:T(8,128)(2,1)} %all-to-all-done), kind=kLoop, calls=%fused_computation.42 | loop fusion | flops 262144 | bytes 1572864
  30.6 0.1 copy.54
  30.7 0.2 copy-done.5
  30.9 0.1 copy-done.7
  31.0 1.2 %multiply_reduce_fusion = (f32[32]{0:T(128)S(1)}, f32[32,8192]{1,0:T(8,128)S(1)}, bf16[32,8192]{1,0:T(8,128)(2,1)}) fusion(bf16[32,8192]{1,0:T(8,128)(2,1)S(1)} %copy-done.1, bf16[32,8192]{1,0:T(8,128)(2,1)S(1)} %copy-done.3, f32[32,8192]{1,0:T(8,128)S(1)} %bitcast.159, bf16[32,8192]{1,0:T(8,128)(2,1)S(1)} %copy-done.7, f32[32,8192]{1,0:T(8,128)S(1)} %bitcast.158), kind=kLoop, calls=%fused_computation.43 | loop fusion | flops 2359264 | bytes 5243008 | tf_op jit(solution)/shard_map/reduce_sum | solution.py:109
  32.3 0.6 copy.55
  32.9 1.7 %fusion.32 = f32[2,16,16,16]{3,2,1,0:T(8,128)} fusion(f32[2,16]{1,0:T(2,128)S(1)} %get-tuple-element.299, f32[2,16,16,512]{3,2,1,0:T(8,128)S(1)} %bitcast.147), kind=kOutput, calls=%fused_computation.35 | convolution fusion | flops 50348032 | bytes 1081472 | tf_op jit(solution)/shard_map/gcni,gri->gcnr/dot_general | solution.py:106
  34.6 1.8 %copy.30 = f32[2,16,16,16]{2,1,3,0:T(8,128)} copy(f32[2,16,16,16]{3,2,1,0:T(8,128)} %fusion.32) | data formatting | bytes 65536 | tf_op jit(solution)/shard_map/gcni,gri->gcnr/dot_general | solution.py:106
  36.4 1.2 %multiply_reduce_fusion.3 = f32[2,16]{1,0:T(2,128)S(1)} fusion(f32[2,16,16,16]{2,1,3,0:T(8,128)} %copy.30, f32[2,16,16,16]{2,1,3,0:T(8,128)} %copy-done.6), kind=kLoop, calls=%fused_computation.59 | loop fusion | flops 16352 | bytes 65664 | tf_op jit(solution)/shard_map/reduce_sum | solution.py:107
  37.6 3.2 %fusion.27 = f32[2,512,512,1]{2,1,3,0:T(8,128)S(1)} fusion(f32[2,16,16,512]{3,2,1,0:T(8,128)} %bitcast.155, f32[2,16,16,512]{3,2,1,0:T(8,128)S(1)} %bitcast.148), kind=kOutput, calls=%fused_computation.29 | convolution fusion | flops 1610612736 | bytes 4194304 | tf_op jit(solution)/shard_map/gcni,gcnj->gij/dot_general | solution.py:102
  40.8 2.0 %fusion.24 = f32[2,16]{1,0:T(2,128)S(1)} fusion(f32[2,512,512,1]{2,1,3,0:T(8,128)S(1)} %fusion.27, pred[512,512]{1,0:T(8,128)(4,1)S(1)} %iota_compare_fusion, f32[2,16]{1,0:T(2,128)S(1)} %copy-done.8, f32[512]{0:T(512)S(1)} %iota_add_fusion.1, f32[2,16]{1,0:T(2,128)S(1)} %get-tuple-element.299), kind=kOutput, calls=%fused_computation.26 | convolution fusion | flops 101253088 | bytes 2361728 | tf_op jit(solution)/shard_map/gij,grj->gri/dot_general | solution.py:104
  42.8 5.2 %all-reduce = (f32[2,16]{1,0:T(2,128)S(1)}, f32[32]{0:T(128)S(1)}) all-reduce(f32[2,16]{1,0:T(2,128)S(1)} %add_multiply_fusion, f32[32]{0:T(128)S(1)} %get-tuple-element.291), channel_id=1, replica_groups=mesh['ctx'=2,'ch'=16] {'ctx'}, use_global_device_ids=true, to_apply=%region_6.7 | all-reduce | flops 64 | bytes 512 | tf_op jit(solution)/shard_map/psum | solution.py:110
  48.0 0.6 broadcast_multiply_fusion
  48.5 0.5 broadcast_multiply_fusion.2
  49.1 1.7 %multiply_reduce_fusion.2 = (f32[2,16,16]{1,2,0:T(8,128)S(1)}, f32[2,16,16,16]{3,2,1,0:T(8,128)}) fusion(f32[2,16,16]{1,2,0:T(8,128)S(1)} %copy.50, f32[512]{0:T(512)S(1)} %iota_add_fusion, f32[2,16]{1,0:T(2,128)S(1)} %get-tuple-element.299, f32[2,16,16,512]{3,2,1,0:T(8,128)S(1)} %bitcast.149), kind=kOutput, calls=%fused_computation.54 | convolution fusion | flops 50363904 | bytes 1087616 | tf_op jit(solution)/shard_map/gcni,gri->gcnr/dot_general | solution.py:73
  50.8 1.8 %copy.24 = f32[2,16,16,16]{2,1,3,0:T(8,128)} copy(f32[2,16,16,16]{3,2,1,0:T(8,128)} %get-tuple-element.306) | data formatting | bytes 65536 | tf_op jit(solution)/shard_map/gcni,gri->gcnr/dot_general | solution.py:73
  52.6 4.4 %all-gather = f32[4,16,16]{2,1,0:T(8,128)S(1)} all-gather(f32[2,16,16]{2,1,0:T(8,128)S(1)} %bitcast.168), channel_id=2, replica_groups=mesh['ctx'=2,'ch'=16] {'ctx'}, dimensions={0}, use_global_device_ids=true | all-gather | bytes 6144 | tf_op jit(solution)/shard_map/all_gather | solution.py:11
  57.0 0.1 while.36
  57.1 0.1 copy.25
  57.2 1.4 %fusion.22 = f32[2,16,16,16]{2,1,3,0:T(8,128)S(1)} fusion(f32[2,16,16,16]{2,1,3,0:T(8,128)} %copy.24, f32[2,16,16]{2,1,0:T(8,128)S(1)} %get-tuple-element.302, f32[2,16,16]{2,1,0:T(8,128)S(1)} %copy.25, f32[16,16]{1,0:T(8,128)S(1)} %fusion.87, f32[2,16]{1,0:T(2,128)S(1)} %get-tuple-element.300, pred[16,16]{1,0:T(8,128)(4,1)S(1)} %fusion.88), kind=kOutput, calls=%fused_computation.24 | convolution fusion | flops 1605632 | bytes 71040 | tf_op jit(solution)/shard_map/grmn,gcmr->gcnr/dot_general | solution.py:90
  58.6 1.0 %fusion.46 = f32[2,16,16,512]{3,2,1,0:T(8,128)S(1)} fusion(f32[2,16,16,16]{2,1,3,0:T(8,128)S(1)} %fusion.22, f32[512]{0:T(512)S(1)} %iota_subtract_fusion.2, f32[2,16]{1,0:T(2,128)S(1)} %get-tuple-element.299, f32[2,16]{1,0:T(2,128)S(1)} %get-tuple-element.296), kind=kOutput, calls=%fused_computation.57 | convolution fusion | flops 50364416 | bytes 1083648 | tf_op jit(solution)/shard_map/gcnr,gri->gcni/dot_general | solution.py:96
  59.6 2.1 %fusion.12 = f32[2,16,16,512]{3,2,1,0:T(8,128)S(1)} fusion(f32[2,16,16,512]{3,2,1,0:T(8,128)S(1)} %fusion.46, f32[2,512,512]{2,1,0:T(8,128)S(1)} %fusion.69, pred[512,512]{1,0:T(8,128)(4,1)S(1)} %iota_compare_fusion, f32[2,16]{1,0:T(2,128)S(1)} %mul.280, f32[2,16,16,512]{3,2,1,0:T(8,128)S(1)} %bitcast.150, f32[2,16,16,512]{3,2,1,0:T(8,128)S(1)} %bitcast.151), kind=kOutput, calls=%fused_computation.15 | convolution fusion | flops 1611923456 | bytes 6553728 | tf_op jit(solution)/shard_map/gcni,gij->gcnj/dot_general | solution.py:72
  61.8 0.6 copy.56
  62.4 0.4 copy-done.2
  62.8 0.2 copy-done.4
  63.0 1.2 %fusion.26 = (bf16[32,8192]{1,0:T(8,128)(2,1)}, bf16[32,8192]{1,0:T(8,128)(2,1)}) fusion(f32[32,8192]{1,0:T(8,128)S(1)} %bitcast.156, bf16[32,8192]{1,0:T(8,128)(2,1)S(1)} %copy-done.4, bf16[32,8192]{1,0:T(8,128)(2,1)S(1)} %copy-done.2), kind=kLoop, calls=%fused_computation.28 | loop fusion | flops 1572864 | bytes 3145728 | tf_op jit(solution)/shard_map/convert_element_type | solution.py:101
  (34 shorter events, 0.2 us)
Async XLA Ops:
  0.6 28.6 %all-to-all-start = ((bf16[16,32,512]{2,1,0:T(8,128)(2,1)}), bf16[16,32,512]{2,1,0:T(8,128)(2,1)}, u32[]{:S(2)}, u32[]{:S(2)}) async-start(bf16[16,32,512]{2,1,0:T(8,128)(2,1)} %bitcast.165), calls=%async_computation | async-start | bytes 1048576 | tf_op jit(solution)/shard_map/all_to_all | solution.py:69
  10.7 10.9 %copy-start.9 = (f32[32]{0:T(128)S(1)}, f32[32]{0:T(128)}, u32[]{:S(2)}) copy-start(f32[32]{0:T(128)} %param.17) | copy-start | bytes 388
  11.3 14.1 %copy-start = (f32[4,8,16,512]{3,2,1,0:T(8,128)}, f32[4,8,16,512]{3,2,1,0:T(8,128)S(1)}, u32[]{:S(2)}) copy-start(f32[4,8,16,512]{3,2,1,0:T(8,128)S(1)} %copy.57) | copy-start | bytes 3145732
  11.3 12.1 %copy-start.8 = (f32[2,16]{1,0:T(2,128)S(1)}, f32[2,16]{1,0:T(2,128)}, u32[]{:S(2)}) copy-start(f32[2,16]{1,0:T(2,128)} %param.16) | copy-start | bytes 388
  22.3 1.1 %copy-start.6 = (f32[2,16,16,16]{2,1,3,0:T(8,128)}, f32[2,16,16,16]{2,1,3,0:T(8,128)S(1)}, u32[]{:S(2)}) copy-start(f32[2,16,16,16]{2,1,3,0:T(8,128)S(1)} %fusion.21) | copy-start | bytes 98308
  29.2 1.5 %copy-start.1 = (bf16[32,8192]{1,0:T(8,128)(2,1)S(1)}, bf16[32,8192]{1,0:T(8,128)(2,1)}, u32[]{:S(2)}) copy-start(bf16[32,8192]{1,0:T(8,128)(2,1)} %param.12) | copy-start | bytes 1572868
  29.2 1.5 %copy-start.3 = (bf16[32,8192]{1,0:T(8,128)(2,1)S(1)}, bf16[32,8192]{1,0:T(8,128)(2,1)}, u32[]{:S(2)}) copy-start(bf16[32,8192]{1,0:T(8,128)(2,1)} %param.11) | copy-start | bytes 1572868
  29.2 1.7 %copy-start.5 = (f32[4,8,16,512]{3,1,2,0:T(8,128)S(1)}, f32[4,8,16,512]{3,1,2,0:T(8,128)}, u32[]{:S(2)}) copy-start(f32[4,8,16,512]{3,1,2,0:T(8,128)} %copy.58) | copy-start | bytes 3145732
  29.2 1.8 %copy-start.7 = (bf16[32,8192]{1,0:T(8,128)(2,1)S(1)}, bf16[32,8192]{1,0:T(8,128)(2,1)}, u32[]{:S(2)}) copy-start(bf16[32,8192]{1,0:T(8,128)(2,1)} %param.13) | copy-start | bytes 1572868
  61.8 1.0 %copy-start.2 = (bf16[32,8192]{1,0:T(8,128)(2,1)S(1)}, bf16[32,8192]{1,0:T(8,128)(2,1)}, u32[]{:S(2)}) copy-start(bf16[32,8192]{1,0:T(8,128)(2,1)} %param.12) | copy-start | bytes 1572868
  61.8 1.2 %copy-start.4 = (bf16[32,8192]{1,0:T(8,128)(2,1)S(1)}, bf16[32,8192]{1,0:T(8,128)(2,1)}, u32[]{:S(2)}) copy-start(bf16[32,8192]{1,0:T(8,128)(2,1)} %param.11) | copy-start | bytes 1572868
where the time goes:
time: 64.6 us; the launch traced here: 64.1 us
  matrix products  20 us (31%)
  blocking collectives  18.4 us (28%)
  local copies, waits for them, and re-layouts  8.62 us (13%)
  other arithmetic  8.56 us (13%)
  starting transfers between devices  7.45 us (12%)
  between operations  0.96 us (1%)
    all_gather x3, blocking collectives, carried_in(): everything = jax.tree.map(lambda part: lax.all_gather(part, axis), array)  13.2 us
    all_to_all x1, starting transfers between devices, on_device(): lax.all_to_all(grad_heads, 'ch', split_axis=0, concat_axis=1, tiled=True)  7.45 us
    psum x1, blocking collectives, on_device(): filter_sum, skip_sum = lax.psum((filter_part, skip_part), 'ctx')  5.16 us
    unnamed x26, local copies, waits for them, and re-layouts  4.57 us
    dot_general x1, matrix products, on_device(): jnp.einsum('gcni,gcnj->gij', grad_split, gated_split, precision=PRECISE)  3.15 us
    dot_general x1, matrix products, on_device(): jnp.einsum('gcnj,gij->gcni', gated_split, toeplitz, precision=PRECISE)  2.16 us
    dot_general x1, matrix products, on_device(): jnp.einsum('gcni,gij->gcnj', grad_split, toeplitz, precision=PRECISE)  2.14 us
    dot_general x1, matrix products, on_device(): folded = jnp.einsum('gij,grj->gri', cross_sums, rising, precision=PRECISE)  1.99 us
  transfers between devices with their start and end apart: 1, of which 0 were waited for; matrix products, arithmetic and copies ran while one was open for 19% of the time, Pallas kernels for 0%

commit v1 on v0

v1 whole, which is shorter than its diff:
```python
import functools

import jax
import jax.numpy as jnp
from jax import lax
from jax.experimental import pallas as pl
from jax.experimental.pallas import tpu as pltpu
from jax.sharding import PartitionSpec as P

MESH = pl.DeviceIdType.MESH
EXACT = lax.Precision.HIGHEST
F32 = jnp.float32
BF16 = jnp.bfloat16


def flip(index, bits):
    out, bit = index, 1
    while bit <= bits:
        if bits & bit:
            out = out + bit * (1 - 2 * lax.rem(lax.div(index, bit), 2))
        bit *= 2
    return out


def interleaved(count):
    far, near = list(range(count - 1, count // 2 - 1, -1)), list(range(count // 2 - 1, 0, -1))
    order = []
    for k in range(len(far)):
        order.append(far[k])
        if k < len(near):
            order.append(near[k])
    return order


def dot(a, b, precision=None):
    return jnp.dot(a, b, precision=precision, preferred_element_type=F32)


def dot_nt(a, b):
    return lax.dot_general(a, b, (((1,), (1,)), ((), ())), preferred_element_type=F32)


def dot_tn(a, b):
    return lax.dot_general(a, b, (((0,), (0,)), ((), ())), preferred_element_type=F32)


def kernel(
    dims,
    first_hbm, second_hbm, third_hbm, heads_hbm, residue_ref, decay_ref, skip_ref,
    out_first, out_second, out_third, out_residue, out_skip,
    first, second, third, heads, x_buf, g_buf, conv, stage_first, stage_second, stage_third,
    toep, enter_buf, leave_buf, fwd_pow, bwd_pow, fwd_slots, bwd_slots, sum_slots,
    load_sem, send_sem, recv_sem, fwd_send, fwd_recv, bwd_send, bwd_recv, sum_send, sum_recv,
    third_sem, first_sem, second_sem,
):
    nch, nctx, channels, length, groups, modes, seq_total = dims
    width = channels // groups
    chunk = length // nch
    span = min(256, length)
    spans = length // span
    unit = max(chunk, span)
    per_unit = unit // chunk
    units = length // unit
    unit_spans = unit // span
    me = lax.axis_index("ch")
    me_x = lax.axis_index("ctx")

    loads = [
        pltpu.make_async_copy(src, dst, load_sem.at[k])
        for k, (src, dst) in enumerate(
            ((first_hbm, first), (second_hbm, second), (third_hbm, third))
        )
    ]
    for load in loads:
        load.start()

    def rows_of(index):
        return pl.ds(pl.multiple_of(index * channels, channels), channels)

    def cols_of(index):
        return pl.ds(pl.multiple_of(index * chunk, chunk), chunk)

    own = pltpu.make_async_copy(
        heads_hbm.at[rows_of(me)], heads.at[:, cols_of(me)], recv_sem.at[me]
    )
    own.start()

    barrier = pltpu.get_barrier_semaphore()
    for s in range(1, nch):
        pl.semaphore_signal(barrier, inc=1, device_id={"ch": flip(me, s)}, device_id_type=MESH)
    for k in range(1, nctx):
        pl.semaphore_signal(
            barrier, inc=1, device_id={"ctx": lax.rem(me_x + k, nctx)}, device_id_type=MESH
        )
    pl.semaphore_wait(barrier, nch - 1 + nctx - 1)

    sends = []
    for s in interleaved(nch):
        to = flip(me, s)
        copy = pltpu.make_async_remote_copy(
            src_ref=heads_hbm.at[rows_of(to)],
            dst_ref=heads.at[:, cols_of(me)],
            send_sem=send_sem.at[s],
            recv_sem=recv_sem.at[me],
            device_id={"ch": to},
            device_id_type=MESH,
        )
        copy.start()
        sends.append(copy)

    def spread(slots, send, recv):
        copies = []
        for k in range(1, nctx):
            copy = pltpu.make_async_remote_copy(
                src_ref=slots.at[me_x],
                dst_ref=slots.at[me_x],
                send_sem=send.at[k],
                recv_sem=recv.at[me_x],
                device_id={"ctx": lax.rem(me_x + k, nctx)},
                device_id_type=MESH,
            )
            copy.start()
            copies.append(copy)
        return copies

    def gather(slots, send, recv):
        for k in range(1, nctx):
            at = lax.rem(me_x + k, nctx)
            pltpu.make_async_remote_copy(
                src_ref=slots.at[at],
                dst_ref=slots.at[at],
                send_sem=send.at[k],
                recv_sem=recv.at[at],
                device_id={"ctx": at},
                device_id_type=MESH,
            ).wait_recv()

    def iota(shape, dim):
        return lax.broadcasted_iota(jnp.int32, shape, dim)

    def column(row):
        size = row.shape[1]
        eye = iota((size, size), 0) == iota((size, size), 1)
        return jnp.sum(jnp.where(eye, jnp.broadcast_to(row, (size, size)), 0.0), axis=1, keepdims=True)

    token_row = iota((modes, span), 1).astype(F32)
    token_col = iota((span, modes), 0).astype(F32)
    middle = float(span // 2)
    lower = iota((span, span), 0) >= iota((span, span), 1)
    span_index = lax.div(iota((spans * width, modes), 0), width).astype(F32)
    rate_row, root_row, span_decay, rise, fall, tail, decay_in = [], [], [], [], [], [], []
    fall_col, rise_col = [], []
    for g in range(groups):
        rate = decay_ref[g : g + 1, :]
        root = jnp.sqrt(2.0 * rate)
        weight = residue_ref[g : g + 1, :] * root
        rate_c, weight_c = column(rate), column(weight)
        rate_row.append(rate)
        root_row.append(root)
        span_decay.append(jnp.exp(-rate * span))
        rise.append(weight_c * jnp.exp(-rate_c * token_row))
        fall.append((weight_c * jnp.exp(-rate_c * (span - 1.0 - token_row))).astype(BF16))
        tail.append(jnp.exp(-rate * (span - token_col)).astype(BF16))
        decay_in.append(jnp.exp(-rate * token_col).astype(BF16))
        fall_col.append(jnp.exp(-rate * (token_col - middle)))
        rise_col.append(jnp.exp(rate * (token_col - middle)).astype(BF16))
        rising = jnp.exp(rate_c * (token_row - middle))
        toeplitz = dot(weight * fall_col[g], rising, EXACT)
        toep[g] = jnp.where(lower, toeplitz, 0.0).astype(BF16)
        fwd_pow[g] = jnp.exp(-rate * span * span_index)
        bwd_pow[g] = jnp.exp(-rate * span * (spans - 1.0 - span_index))
    skip_col = column(skip_ref[...])

    loads[0].wait()
    loads[1].wait()

    def gate(n, carry):
        at = pl.ds(pl.multiple_of(n * span, span), span)
        gated = (first[:, at].astype(F32) * second[:, at].astype(F32)).astype(BF16)
        for g in range(groups):
            x_buf[g, pl.ds(pl.multiple_of(n * width, width), width), :] = gated[
                g * width : (g + 1) * width
            ]
        return carry

    lax.fori_loop(0, spans, gate, 0)

    for g in range(groups):
        state = dot(x_buf[g], tail[g])
        run = jnp.zeros((width, modes), F32)
        for n in range(spans):
            at = slice(n * width, (n + 1) * width)
            enter_buf[g, at, :] = run
            run = run * span_decay[g] + state[at]
        fwd_slots[me_x, g * width : (g + 1) * width, :] = run
    fwd_copies = spread(fwd_slots, fwd_send, fwd_recv)
    for g in range(groups):
        conv[g] = dot_nt(x_buf[g], toep[g])
    gather(fwd_slots, fwd_send, fwd_recv)

    def entering(slots, g, before):
        total = jnp.zeros((width, modes), F32)
        for k in range(nctx):
            gap = me_x - 1 - k if before else k - 1 - me_x
            steps = jnp.maximum(gap, 0).astype(F32)
            decayed = slots[k, g * width : (g + 1) * width, :] * jnp.exp(
                -rate_row[g] * length * steps
            )
            total = total + jnp.where(gap >= 0, decayed, 0.0)
        return jnp.concatenate([total] * spans, axis=0)

    for g in range(groups):
        enter = enter_buf[g] + fwd_pow[g] * entering(fwd_slots, g, True)
        enter_buf[g] = enter
        skips = jnp.concatenate([skip_col[g * width : (g + 1) * width]] * spans, axis=0)
        conv[g] = conv[g] + dot(enter, rise[g], EXACT) + skips * x_buf[g].astype(F32)

    loads[2].wait()
    skip_sum = jnp.zeros((channels, span), F32)
    third_copies = []
    order = [0] + interleaved(units) if units > 1 else [0]
    for s in order:
        at_unit = flip(lax.div(me, per_unit), s)
        for q in range(per_unit):
            src = at_unit * per_unit + q
            pltpu.make_async_copy(
                heads_hbm.at[rows_of(0)], heads.at[:, cols_of(src)], recv_sem.at[src]
            ).wait()
        for q in range(unit_spans):
            n = at_unit * unit_spans + q
            cols = pl.ds(pl.multiple_of(n * span, span), span)
            rows = pl.ds(pl.multiple_of(n * width, width), width)
            out_grad = heads[:, cols].astype(F32)
            grad = out_grad * third[:, cols].astype(F32)
            gated = jnp.concatenate([x_buf[g, rows, :] for g in range(groups)], axis=0)
            convolved = jnp.concatenate([conv[g, rows, :] for g in range(groups)], axis=0)
            skip_sum = skip_sum + grad * gated.astype(F32)
            stage_third[:, cols] = (out_grad * convolved).astype(BF16)
            rounded = grad.astype(BF16)
            for g in range(groups):
                g_buf[g, rows, :] = rounded[g * width : (g + 1) * width]
        cols = pl.ds(pl.multiple_of(at_unit * unit, unit), unit)
        copy = pltpu.make_async_copy(
            stage_third.at[:, cols], out_third.at[:, cols], third_sem.at[s]
        )
        copy.start()
        third_copies.append(copy)

    far = []
    for g in range(groups):
        weighted = dot(g_buf[g], decay_in[g])
        far.append(jnp.sum(weighted * enter_buf[g], axis=0, keepdims=True))
        state = weighted * jnp.exp(-rate_row[g])
        run = jnp.zeros((width, modes), F32)
        for n in reversed(range(spans)):
            at = slice(n * width, (n + 1) * width)
            leave_buf[g, at, :] = run
            run = run * span_decay[g] + state[at]
        bwd_slots[me_x, g * width : (g + 1) * width, :] = run
    bwd_copies = spread(bwd_slots, bwd_send, bwd_recv)

    sum_slots[me_x] = jnp.zeros(sum_slots.shape[1:], F32)
    for g in range(groups):
        cross = jnp.where(lower, dot_tn(g_buf[g], x_buf[g]), 0.0).astype(BF16)
        near = jnp.sum(dot(cross, rise_col[g]) * fall_col[g], axis=0, keepdims=True)
        sum_slots[me_x, g : g + 1, 0:modes] = root_row[g] * (near + far[g])
    skip_total = jnp.sum(skip_sum, axis=1, keepdims=True)
    eye = iota((channels, channels), 0) == iota((channels, channels), 1)
    sum_slots[me_x, groups : groups + 1, 0:channels] = jnp.sum(
        jnp.where(eye, jnp.broadcast_to(skip_total, (channels, channels)), 0.0),
        axis=0,
        keepdims=True,
    )
    sum_copies = spread(sum_slots, sum_send, sum_recv)
    for g in range(groups):
        skips = jnp.concatenate([skip_col[g * width : (g + 1) * width]] * spans, axis=0)
        conv[g] = dot(g_buf[g], toep[g]) + skips * g_buf[g].astype(F32)

    gather(bwd_slots, bwd_send, bwd_recv)
    for g in range(groups):
        leave_buf[g] = leave_buf[g] + bwd_pow[g] * entering(bwd_slots, g, False)
    pieces = 4 if spans % 4 == 0 else 1
    piece_spans = spans // pieces
    out_copies = []
    for p in range(pieces):
        for g in range(groups):
            rows = slice(p * piece_spans * width, (p + 1) * piece_spans * width)
            mixed = conv[g, rows, :] + dot(leave_buf[g, rows, :].astype(BF16), fall[g])
            for q in range(piece_spans):
                n = p * piece_spans + q
                part = mixed[q * width : (q + 1) * width]
                at = (slice(g * width, (g + 1) * width), slice(n * span, (n + 1) * span))
                stage_first[at] = (part * second[at].astype(F32)).astype(BF16)
                stage_second[at] = (part * first[at].astype(F32)).astype(BF16)
        cols = pl.ds(p * piece_spans * span, piece_spans * span)
        for stage, out, sem in (
            (stage_first, out_first, first_sem),
            (stage_second, out_second, second_sem),
        ):
            copy = pltpu.make_async_copy(stage.at[:, cols], out.at[:, cols], sem.at[p])
            copy.start()
            out_copies.append(copy)

    gather(sum_slots, sum_send, sum_recv)
    total = sum_slots[0]
    for k in range(1, nctx):
        total = total + sum_slots[k]
    out_residue[...] = total[0:groups, 0:modes] / jnp.sqrt(F32(width * seq_total))
    out_skip[...] = total[groups : groups + 1, 0:channels] / jnp.sqrt(F32(seq_total))

    for copy in sends + fwd_copies + bwd_copies + sum_copies:
        copy.wait_send()
    for copy in third_copies + out_copies:
        copy.wait()


def on_device(nch, nctx, first_in, second_in, third_in, grad_heads, residue, decay_rate, skip_gain):
    channels, length = first_in.shape
    groups, modes = residue.shape
    width = channels // groups
    span = min(256, length)
    spans = length // span
    units = length // max(length // nch, span)
    dims = (nch, nctx, channels, length, groups, modes, length * nctx)
    whole, vmem = pl.BlockSpec(memory_space=pl.ANY), pl.BlockSpec(memory_space=pltpu.VMEM)
    big = jax.ShapeDtypeStruct((channels, length), BF16)
    big_buf = pltpu.VMEM((channels, length), BF16)
    half_buf = pltpu.VMEM((groups, spans * width, span), BF16)
    state_buf = pltpu.VMEM((groups, spans * width, modes), F32)
    slots = pltpu.VMEM((nctx, channels, modes), F32)
    dma = pltpu.SemaphoreType.DMA
    outs = pl.pallas_call(
        functools.partial(kernel, dims),
        out_shape=(
            big, big, big,
            jax.ShapeDtypeStruct((groups, modes), F32),
            jax.ShapeDtypeStruct((1, channels), F32),
        ),
        in_specs=[whole] * 4 + [vmem] * 3,
        out_specs=[whole] * 3 + [vmem] * 2,
        scratch_shapes=[
            big_buf, big_buf, big_buf, big_buf,
            half_buf, half_buf,
            pltpu.VMEM((groups, spans * width, span), F32),
            big_buf, big_buf, big_buf,
            pltpu.VMEM((groups, span, span), BF16),
            state_buf, state_buf, state_buf, state_buf,
            slots, slots,
            pltpu.VMEM((nctx, 8, 128), F32),
            dma((3,)),
            dma((nch,)), dma((nch,)),
            dma((nctx,)), dma((nctx,)), dma((nctx,)), dma((nctx,)), dma((nctx,)), dma((nctx,)),
            dma((units,)), dma((4,)), dma((4,)),
        ],
        compiler_params=pltpu.CompilerParams(
            collective_id=0, has_side_effects=True, vmem_limit_bytes=40 * 1024 * 1024
        ),
        cost_estimate=pl.CostEstimate(
            flops=12 * channels * length * span, bytes_accessed=14 * channels * length,
            transcendentals=0,
        ),
    )(
        first_in, second_in, third_in, grad_heads, residue, decay_rate,
        skip_gain.reshape(1, channels),
    )
    return (*outs[:4], outs[4].reshape(channels))


def solution(mesh):
    return jax.shard_map(
        functools.partial(on_device, mesh.shape["ch"], mesh.shape["ctx"]),
        mesh=mesh,
        in_specs=(
            P("ch", "ctx"),
            P("ch", "ctx"),
            P("ch", "ctx"),
            P(None, ("ctx", "ch")),
            P("ch", None),
            P("ch", None),
            P("ch"),
        ),
        out_specs=(P("ch", "ctx"), P("ch", "ctx"), P("ch", "ctx"), P("ch", None), P("ch")),
        check_vma=False,
    )
```

time: 64.6 us -> 34.4 us (0.53)
  Pallas kernels: 0 us -> 24.4 us
  matrix products: 20 us -> 0 us
  blocking collectives: 18.4 us -> 0 us
  other arithmetic: 8.56 us -> 0 us
  starting transfers between devices: 7.45 us -> 0 us
    pallas_call x0 -> x1, Pallas kernels: none -> 24.4 us  [on_device(): pl.pallas_call(functools.partial(kernel, dims), out_shape=(big, big, big,...]
    dot_general x12 -> x0, matrix products: 20 us -> none  [the longest x1 3.15 us: on_device(): jnp.einsum('gcni,gcnj->gij', grad_split, gated_split, precision=PRECISE)]
    all_gather x3 -> x0, blocking collectives: 13.2 us -> none  [carried_in(): everything = jax.tree.map(lambda part: lax.all_gather(part, axis), array)]
    all_to_all x1 -> x0, starting transfers between devices: 7.45 us -> none  [on_device(): lax.all_to_all(grad_heads, 'ch', split_axis=0, concat_axis=1, tiled=True)]
    psum x1 -> x0, blocking collectives: 5.16 us -> none  [on_device(): filter_sum, skip_sum = lax.psum((filter_part, skip_part), 'ctx')]
    unnamed x26 -> x19, local copies, waits for them, and re-layouts: 4.57 us -> 8.98 us
    dot_general x3 -> x0, local copies, waits for them, and re-layouts: 3.73 us -> none  [the longest x1 1.79 us: on_device(): jnp.einsum('gcni,gri->gcnr', grad_split, decay_in, precision=PRECISE)]
    reduce_sum x2 -> x0, other arithmetic: 2.46 us -> none  [the longest x1 1.23 us: on_device(): far_part = jnp.sum(weighted * enter_spans, axis=(1, 2))]
  transfers between devices with their start and end apart: 1 -> 0, of which waited for: 0 -> 0; matrix products, arithmetic and copies ran while one was open for 19% -> 0% of each run, Pallas kernels for 0% -> 0%
where the time goes in v1:
time: 34.4 us; the launch traced here: 34 us
  Pallas kernels  24.4 us (71%)
  local copies, waits for them, and re-layouts  8.98 us (26%)
  between operations  0.67 us (2%)
    pallas_call x1, Pallas kernels, on_device(): pl.pallas_call(functools.partial(kernel, dims), out_shape=(big, big, big,...  24.4 us
    unnamed x19, local copies, waits for them, and re-layouts  8.98 us

profile of v1, /device:TPU:0, one launch (start us, length us, event | category | flops | bytes accessed | tf_op | source)
XLA Modules:
  0.0 34.0 jit_solution(10961088977215061655)
XLA Ops:
  0.6 0.0 copy-start.6
  0.6 0.0 copy-start.4
  0.7 0.6 %copy-done.6 = f32[32]{0:T(128)S(1)} copy-done((f32[32]{0:T(128)S(1)}, f32[32]{0:T(128)}, u32[]{:S(2)}) %copy-start.6) | copy-done | bytes 152
  1.3 0.0 copy-done.4
  1.3 0.0 copy-start
  1.3 1.0 %copy-done = bf16[32,8192]{1,0:T(8,128)(2,1)S(1)} copy-done((bf16[32,8192]{1,0:T(8,128)(2,1)S(1)}, bf16[32,8192]{1,0:T(8,128)(2,1)}, u32[]{:S(2)}) %copy-start) | copy-done | bytes 524312
  2.4 0.0 copy-start.1
  2.4 1.0 %copy-done.1 = bf16[32,8192]{1,0:T(8,128)(2,1)S(1)} copy-done((bf16[32,8192]{1,0:T(8,128)(2,1)S(1)}, bf16[32,8192]{1,0:T(8,128)(2,1)}, u32[]{:S(2)}) %copy-start.1) | copy-done | bytes 524312
  3.4 0.0 copy-start.2
  3.4 1.0 %copy-done.2 = bf16[32,8192]{1,0:T(8,128)(2,1)S(1)} copy-done((bf16[32,8192]{1,0:T(8,128)(2,1)S(1)}, bf16[32,8192]{1,0:T(8,128)(2,1)}, u32[]{:S(2)}) %copy-start.2) | copy-done | bytes 524312
  4.5 0.0 copy-start.3
  4.5 1.0 %copy-done.3 = bf16[512,512]{1,0:T(8,128)(2,1)S(1)} copy-done((bf16[512,512]{1,0:T(8,128)(2,1)S(1)}, bf16[512,512]{1,0:T(8,128)(2,1)}, u32[]{:S(2)}) %copy-start.3) | copy-done | bytes 524312
  5.5 0.0 copy-start.5
  5.5 0.7 %copy-done.5 = f32[2,16]{1,0:T(2,128)S(1)} copy-done((f32[2,16]{1,0:T(2,128)S(1)}, f32[2,16]{1,0:T(2,128)}, u32[]{:S(2)}) %copy-start.5) | copy-done | bytes 152
  6.2 24.4 %shard_map.110 = (bf16[32,8192]{1,0:T(8,128)(2,1)S(1)}, bf16[32,8192]{1,0:T(8,128)(2,1)S(1)}, bf16[32,8192]{1,0:T(8,128)(2,1)S(1)}, f32[2,16]{1,0:T(2,128)S(1)}, f32[1,32]{1,0:T(1,128)S(1)}) custom-call(bf16[32,8192]{1,0:T(8,128)(2,1)S(1)} %copy-done, bf16[32,8192]{1,0:T(8,128)(2,1)S(1)} %copy-done.1, bf16[32,8192]{1,0:T(8,128)(2,1)S(1)} %copy-done.2, ...), custom_call_target="tpu_custom_call" | custom-call | flops 805306368 | bytes 3670016 | tf_op jit(solution)/shard_map/pallas_call | solution.py:332
  30.6 0.8 %copy.17 = bf16[32,8192]{1,0:T(8,128)(2,1)} copy(bf16[32,8192]{1,0:T(8,128)(2,1)S(1)} %get-tuple-element.20) | data formatting | bytes 1048576
  31.4 0.8 %copy.18 = bf16[32,8192]{1,0:T(8,128)(2,1)} copy(bf16[32,8192]{1,0:T(8,128)(2,1)S(1)} %get-tuple-element.21) | data formatting | bytes 1048576
  32.2 0.8 %copy.19 = bf16[32,8192]{1,0:T(8,128)(2,1)} copy(bf16[32,8192]{1,0:T(8,128)(2,1)S(1)} %get-tuple-element.22) | data formatting | bytes 1048576
  33.0 0.6 %copy.20 = f32[2,16]{1,0:T(2,128)} copy(f32[2,16]{1,0:T(2,128)S(1)} %get-tuple-element.23) | data formatting | bytes 256
  33.5 0.5 %copy.21 = f32[32]{0:T(128)} copy(f32[32]{0:T(128)S(1)} %bitcast.3) | data formatting | bytes 256
Async XLA Ops:
  0.6 0.7 %copy-start.6 = (f32[32]{0:T(128)S(1)}, f32[32]{0:T(128)}, u32[]{:S(2)}) copy-start(f32[32]{0:T(128)} %param.13) | copy-start | bytes 388
  0.6 0.7 %copy-start.4 = (f32[2,16]{1,0:T(2,128)S(1)}, f32[2,16]{1,0:T(2,128)}, u32[]{:S(2)}) copy-start(f32[2,16]{1,0:T(2,128)} %residue_ref.1) | copy-start | bytes 388
  1.3 1.0 %copy-start = (bf16[32,8192]{1,0:T(8,128)(2,1)S(1)}, bf16[32,8192]{1,0:T(8,128)(2,1)}, u32[]{:S(2)}) copy-start(bf16[32,8192]{1,0:T(8,128)(2,1)} %first_hbm.1) | copy-start | bytes 1572868
  2.4 1.0 %copy-start.1 = (bf16[32,8192]{1,0:T(8,128)(2,1)S(1)}, bf16[32,8192]{1,0:T(8,128)(2,1)}, u32[]{:S(2)}) copy-start(bf16[32,8192]{1,0:T(8,128)(2,1)} %second_hbm.1) | copy-start | bytes 1572868
  3.4 1.0 %copy-start.2 = (bf16[32,8192]{1,0:T(8,128)(2,1)S(1)}, bf16[32,8192]{1,0:T(8,128)(2,1)}, u32[]{:S(2)}) copy-start(bf16[32,8192]{1,0:T(8,128)(2,1)} %third_hbm.1) | copy-start | bytes 1572868
  4.5 1.0 %copy-start.3 = (bf16[512,512]{1,0:T(8,128)(2,1)S(1)}, bf16[512,512]{1,0:T(8,128)(2,1)}, u32[]{:S(2)}) copy-start(bf16[512,512]{1,0:T(8,128)(2,1)} %heads_hbm.1) | copy-start | bytes 1572868
  5.5 0.7 %copy-start.5 = (f32[2,16]{1,0:T(2,128)S(1)}, f32[2,16]{1,0:T(2,128)}, u32[]{:S(2)}) copy-start(f32[2,16]{1,0:T(2,128)} %decay_ref.1) | copy-start | bytes 388

commit v2 on v1

--- a/solution.py
+++ b/solution.py
@@ -23,7 +23,7 @@
 
 
 def interleaved(count):
-    far, near = list(range(count - 1, count // 2 - 1, -1)), list(range(count // 2 - 1, 0, -1))
+    far, near = list(range(count // 2, count)), list(range(1, count // 2))
     order = []
     for k in range(len(far)):
         order.append(far[k])
@@ -46,33 +46,39 @@
 
 def kernel(
     dims,
-    first_hbm, second_hbm, third_hbm, heads_hbm, residue_ref, decay_ref, skip_ref,
-    out_first, out_second, out_third, out_residue, out_skip,
-    first, second, third, heads, x_buf, g_buf, conv, stage_first, stage_second, stage_third,
+    first_hbm, second_hbm, third_hbm, heads_hbm, residue_hbm, decay_hbm, skip_hbm,
+    stage_first, stage_second, stage_third, out_residue, out_skip,
+    first, second, third, heads, x_buf, g_buf, conv, cross_buf,
     toep, enter_buf, leave_buf, fwd_pow, bwd_pow, fwd_slots, bwd_slots, sum_slots,
+    residue_ref, decay_ref, skip_ref,
     load_sem, send_sem, recv_sem, fwd_send, fwd_recv, bwd_send, bwd_recv, sum_send, sum_recv,
-    third_sem, first_sem, second_sem,
 ):
     nch, nctx, channels, length, groups, modes, seq_total = dims
     width = channels // groups
     chunk = length // nch
     span = min(256, length)
     spans = length // span
-    unit = max(chunk, span)
-    per_unit = unit // chunk
-    units = length // unit
-    unit_spans = unit // span
+    batches = 4 if nch % 4 == 0 and spans % 4 == 0 else 1
+    batch_srcs = nch // batches
+    batch_spans = spans // batches
     me = lax.axis_index("ch")
     me_x = lax.axis_index("ctx")
 
     loads = [
         pltpu.make_async_copy(src, dst, load_sem.at[k])
         for k, (src, dst) in enumerate(
-            ((first_hbm, first), (second_hbm, second), (third_hbm, third))
+            (
+                (first_hbm, first),
+                (second_hbm, second),
+                (third_hbm, third),
+                (residue_hbm, residue_ref),
+                (decay_hbm, decay_ref),
+                (skip_hbm, skip_ref),
+            )
         )
     ]
-    for load in loads:
-        load.start()
+    for k in (4, 3, 5, 0, 1):
+        loads[k].start()
 
     def rows_of(index):
         return pl.ds(pl.multiple_of(index * channels, channels), channels)
@@ -83,7 +89,6 @@
     own = pltpu.make_async_copy(
         heads_hbm.at[rows_of(me)], heads.at[:, cols_of(me)], recv_sem.at[me]
     )
-    own.start()
 
     barrier = pltpu.get_barrier_semaphore()
     for s in range(1, nch):
@@ -107,6 +112,8 @@
         )
         copy.start()
         sends.append(copy)
+    own.start()
+    loads[2].start()
 
     def spread(slots, send, recv):
         copies = []
@@ -143,6 +150,8 @@
         eye = iota((size, size), 0) == iota((size, size), 1)
         return jnp.sum(jnp.where(eye, jnp.broadcast_to(row, (size, size)), 0.0), axis=1, keepdims=True)
 
+    for k in (4, 3, 5):
+        loads[k].wait()
     token_row = iota((modes, span), 1).astype(F32)
     token_col = iota((span, modes), 0).astype(F32)
     middle = float(span // 2)
@@ -216,18 +225,20 @@
         conv[g] = conv[g] + dot(enter, rise[g], EXACT) + skips * x_buf[g].astype(F32)
 
     loads[2].wait()
+    batch_rows = batch_spans * width
     skip_sum = jnp.zeros((channels, span), F32)
-    third_copies = []
-    order = [0] + interleaved(units) if units > 1 else [0]
-    for s in order:
-        at_unit = flip(lax.div(me, per_unit), s)
-        for q in range(per_unit):
-            src = at_unit * per_unit + q
+    far_sum = [jnp.zeros((batch_rows, modes), F32) for _ in range(groups)]
+    bwd_sum = [jnp.zeros((batch_rows, modes), F32) for _ in range(groups)]
+    bwd_copies = []
+    for k in range(batches):
+        at_batch = flip(lax.div(me, batch_srcs), k)
+        for q in range(batch_srcs):
+            src = at_batch * batch_srcs + q
             pltpu.make_async_copy(
                 heads_hbm.at[rows_of(0)], heads.at[:, cols_of(src)], recv_sem.at[src]
             ).wait()
-        for q in range(unit_spans):
-            n = at_unit * unit_spans + q
+        for q in range(batch_spans):
+            n = at_batch * batch_spans + q
             cols = pl.ds(pl.multiple_of(n * span, span), span)
             rows = pl.ds(pl.multiple_of(n * width, width), width)
             out_grad = heads[:, cols].astype(F32)
@@ -239,31 +250,33 @@
             rounded = grad.astype(BF16)
             for g in range(groups):
                 g_buf[g, rows, :] = rounded[g * width : (g + 1) * width]
-        cols = pl.ds(pl.multiple_of(at_unit * unit, unit), unit)
-        copy = pltpu.make_async_copy(
-            stage_third.at[:, cols], out_third.at[:, cols], third_sem.at[s]
-        )
-        copy.start()
-        third_copies.append(copy)
-
-    far = []
-    for g in range(groups):
-        weighted = dot(g_buf[g], decay_in[g])
-        far.append(jnp.sum(weighted * enter_buf[g], axis=0, keepdims=True))
-        state = weighted * jnp.exp(-rate_row[g])
-        run = jnp.zeros((width, modes), F32)
-        for n in reversed(range(spans)):
-            at = slice(n * width, (n + 1) * width)
-            leave_buf[g, at, :] = run
-            run = run * span_decay[g] + state[at]
-        bwd_slots[me_x, g * width : (g + 1) * width, :] = run
-    bwd_copies = spread(bwd_slots, bwd_send, bwd_recv)
+        rows = pl.ds(pl.multiple_of(at_batch * batch_rows, batch_rows), batch_rows)
+        for g in range(groups):
+            weighted = dot(g_buf[g, rows, :], decay_in[g])
+            far_sum[g] = far_sum[g] + weighted * enter_buf[g, rows, :]
+            state = weighted * jnp.exp(-rate_row[g])
+            leave_buf[g, rows, :] = state
+            bwd_sum[g] = bwd_sum[g] + state * fwd_pow[g, rows, :]
+        if k == batches - 1:
+            for g in range(groups):
+                run = bwd_sum[g][0:width]
+                for q in range(1, batch_spans):
+                    run = run + bwd_sum[g][q * width : (q + 1) * width]
+                bwd_slots[me_x, g * width : (g + 1) * width, :] = run
+            bwd_copies = spread(bwd_slots, bwd_send, bwd_recv)
+        for g in range(groups):
+            part = g_buf[g, rows, :]
+            skips = jnp.concatenate([skip_col[g * width : (g + 1) * width]] * batch_spans, axis=0)
+            conv[g, rows, :] = dot(part, toep[g]) + skips * part.astype(F32)
+            cross = dot_tn(part, x_buf[g, rows, :])
+            cross_buf[g] = cross if k == 0 else cross_buf[g] + cross
 
     sum_slots[me_x] = jnp.zeros(sum_slots.shape[1:], F32)
     for g in range(groups):
-        cross = jnp.where(lower, dot_tn(g_buf[g], x_buf[g]), 0.0).astype(BF16)
+        cross = jnp.where(lower, cross_buf[g], 0.0).astype(BF16)
         near = jnp.sum(dot(cross, rise_col[g]) * fall_col[g], axis=0, keepdims=True)
-        sum_slots[me_x, g : g + 1, 0:modes] = root_row[g] * (near + far[g])
+        far = jnp.sum(far_sum[g], axis=0, keepdims=True)
+        sum_slots[me_x, g : g + 1, 0:modes] = root_row[g] * (near + far)
     skip_total = jnp.sum(skip_sum, axis=1, keepdims=True)
     eye = iota((channels, channels), 0) == iota((channels, channels), 1)
     sum_slots[me_x, groups : groups + 1, 0:channels] = jnp.sum(
@@ -272,16 +285,19 @@
         keepdims=True,
     )
     sum_copies = spread(sum_slots, sum_send, sum_recv)
-    for g in range(groups):
-        skips = jnp.concatenate([skip_col[g * width : (g + 1) * width]] * spans, axis=0)
-        conv[g] = dot(g_buf[g], toep[g]) + skips * g_buf[g].astype(F32)
+    runs = [jnp.zeros((width, modes), F32) for _ in range(groups)]
+    for n in reversed(range(spans)):
+        at = slice(n * width, (n + 1) * width)
+        for g in range(groups):
+            state = leave_buf[g, at, :]
+            leave_buf[g, at, :] = runs[g]
+            runs[g] = runs[g] * span_decay[g] + state
 
     gather(bwd_slots, bwd_send, bwd_recv)
     for g in range(groups):
         leave_buf[g] = leave_buf[g] + bwd_pow[g] * entering(bwd_slots, g, False)
     pieces = 4 if spans % 4 == 0 else 1
     piece_spans = spans // pieces
-    out_copies = []
     for p in range(pieces):
         for g in range(groups):
             rows = slice(p * piece_spans * width, (p + 1) * piece_spans * width)
@@ -292,14 +308,6 @@
                 at = (slice(g * width, (g + 1) * width), slice(n * span, (n + 1) * span))
                 stage_first[at] = (part * second[at].astype(F32)).astype(BF16)
                 stage_second[at] = (part * first[at].astype(F32)).astype(BF16)
-        cols = pl.ds(p * piece_spans * span, piece_spans * span)
-        for stage, out, sem in (
-            (stage_first, out_first, first_sem),
-            (stage_second, out_second, second_sem),
-        ):
-            copy = pltpu.make_async_copy(stage.at[:, cols], out.at[:, cols], sem.at[p])
-            copy.start()
-            out_copies.append(copy)
 
     gather(sum_slots, sum_send, sum_recv)
     total = sum_slots[0]
@@ -310,7 +318,22 @@
 
     for copy in sends + fwd_copies + bwd_copies + sum_copies:
         copy.wait_send()
-    for copy in third_copies + out_copies:
+
+
+def flush(first, second, third, residue, skip, out_first, out_second, out_third, out_residue, out_skip, sem):
+    length = first.shape[1]
+    pieces = 4 if length % 512 == 0 else 1
+    step = length // pieces
+    copies = []
+    for p in range(pieces):
+        cols = pl.ds(p * step, step)
+        for src, dst in ((first, out_first), (second, out_second), (third, out_third)):
+            copies.append((src.at[:, cols], dst.at[:, cols]))
+    copies += [(residue, out_residue), (skip, out_skip)]
+    copies = [pltpu.make_async_copy(src, dst, sem.at[k]) for k, (src, dst) in enumerate(copies)]
+    for copy in copies:
+        copy.start()
+    for copy in copies:
         copy.wait()
 
 
@@ -320,49 +343,64 @@
     width = channels // groups
     span = min(256, length)
     spans = length // span
-    units = length // max(length // nch, span)
     dims = (nch, nctx, channels, length, groups, modes, length * nctx)
-    whole, vmem = pl.BlockSpec(memory_space=pl.ANY), pl.BlockSpec(memory_space=pltpu.VMEM)
+    whole, vmem = pl.BlockSpec(memory_space=pltpu.HBM), pl.BlockSpec(memory_space=pltpu.VMEM)
     big = jax.ShapeDtypeStruct((channels, length), BF16)
     big_buf = pltpu.VMEM((channels, length), BF16)
     half_buf = pltpu.VMEM((groups, spans * width, span), BF16)
     state_buf = pltpu.VMEM((groups, spans * width, modes), F32)
     slots = pltpu.VMEM((nctx, channels, modes), F32)
     dma = pltpu.SemaphoreType.DMA
+    out_shape = (
+        big, big, big,
+        jax.ShapeDtypeStruct((groups, modes), F32),
+        jax.ShapeDtypeStruct((1, channels), F32),
+    )
     outs = pl.pallas_call(
         functools.partial(kernel, dims),
-        out_shape=(
-            big, big, big,
-            jax.ShapeDtypeStruct((groups, modes), F32),
-            jax.ShapeDtypeStruct((1, channels), F32),
-        ),
-        in_specs=[whole] * 4 + [vmem] * 3,
-        out_specs=[whole] * 3 + [vmem] * 2,
+        out_shape=out_shape,
+        in_specs=[whole] * 7,
+        out_specs=[vmem] * 5,
         scratch_shapes=[
             big_buf, big_buf, big_buf, big_buf,
             half_buf, half_buf,
             pltpu.VMEM((groups, spans * width, span), F32),
-            big_buf, big_buf, big_buf,
+            pltpu.VMEM((groups, span, span), F32),
             pltpu.VMEM((groups, span, span), BF16),
             state_buf, state_buf, state_buf, state_buf,
             slots, slots,
             pltpu.VMEM((nctx, 8, 128), F32),
-            dma((3,)),
+            pltpu.VMEM((groups, modes), F32),
+            pltpu.VMEM((groups, modes), F32),
+            pltpu.VMEM((1, channels), F32),
+            dma((6,)),
             dma((nch,)), dma((nch,)),
             dma((nctx,)), dma((nctx,)), dma((nctx,)), dma((nctx,)), dma((nctx,)), dma((nctx,)),
-            dma((units,)), dma((4,)), dma((4,)),
         ],
         compiler_params=pltpu.CompilerParams(
-            collective_id=0, has_side_effects=True, vmem_limit_bytes=40 * 1024 * 1024
+            collective_id=0, has_side_effects=True, vmem_limit_bytes=32 * 1024 * 1024
         ),
         cost_estimate=pl.CostEstimate(
             flops=12 * channels * length * span, bytes_accessed=14 * channels * length,
             transcendentals=0,
         ),
     )(
-        first_in, second_in, third_in, grad_heads, residue, decay_rate,
-        skip_gain.reshape(1, channels),
+        *(
+            pltpu.with_memory_space_constraint(part, pltpu.HBM)
+            for part in (
+                first_in, second_in, third_in, grad_heads, residue, decay_rate,
+                skip_gain.reshape(1, channels),
+            )
+        )
     )
+    outs = pl.pallas_call(
+        flush,
+        out_shape=out_shape,
+        in_specs=[vmem] * 5,
+        out_specs=[whole] * 5,
+        scratch_shapes=[dma((14,))],
+        compiler_params=pltpu.CompilerParams(vmem_limit_bytes=8 * 1024 * 1024),
+    )(*outs)
     return (*outs[:4], outs[4].reshape(channels))
 
 

time: 34.4 us -> 22.9 us (0.67)
  the two profiles are of different devices: /device:TPU:0 before, /device:TPU:8 now
where the time goes in v2:
time: 22.9 us; the launch traced here: 22.7 us
  Pallas kernels  22.1 us (97%)
  between operations  0.64 us (3%)
    pallas_call x1, Pallas kernels, on_device(): pl.pallas_call(functools.partial(kernel, dims), out_shape=out_shape, in_s...  20.8 us
    pallas_call x1, Pallas kernels, on_device(): pl.pallas_call(flush, out_shape=out_shape, in_specs=[vmem] * 5, out_specs...  1.26 us

profile of v2, /device:TPU:8, one launch (start us, length us, event | category | flops | bytes accessed | tf_op | source)
XLA Modules:
  0.0 22.7 jit_solution(1947001954894023564)
XLA Ops:
  0.6 20.8 %shard_map.110 = (bf16[32,8192]{1,0:T(8,128)(2,1)S(1)}, bf16[32,8192]{1,0:T(8,128)(2,1)S(1)}, bf16[32,8192]{1,0:T(8,128)(2,1)S(1)}, f32[2,16]{1,0:T(2,128)S(1)}, f32[1,32]{1,0:T(1,128)S(1)}) custom-call(bf16[32,8192]{1,0:T(8,128)(2,1)} %first_hbm.1, bf16[32,8192]{1,0:T(8,128)(2,1)} %second_hbm.1, bf16[32,8192]{1,0:T(8,128)(2,1)} %third_hbm.1, ...), custom_call_target="tpu_custom_call" | custom-call | flops 805306368 | bytes 3670016 | tf_op jit(solution)/shard_map/pallas_call | solution.py:359
  21.5 1.3 %shard_map.111 = (bf16[32,8192]{1,0:T(8,128)(2,1)}, bf16[32,8192]{1,0:T(8,128)(2,1)}, bf16[32,8192]{1,0:T(8,128)(2,1)}, f32[2,16]{1,0:T(2,128)}, f32[1,32]{1,0:T(1,128)}) custom-call(bf16[32,8192]{1,0:T(8,128)(2,1)S(1)} %get-tuple-element.15.first, bf16[32,8192]{1,0:T(8,128)(2,1)S(1)} %get-tuple-element.16.second, ...), custom_call_target="tpu_custom_call" | custom-call | tf_op jit(solution)/shard_map/pallas_call | solution.py:396

commit v3 on v2

v3 whole, which is shorter than its diff:
```python
import functools

import jax
import jax.numpy as jnp
from jax import lax
from jax.experimental import pallas as pl
from jax.experimental.pallas import tpu as pltpu
from jax.sharding import PartitionSpec as P

MESH = pl.DeviceIdType.MESH
EXACT = lax.Precision.HIGHEST
F32 = jnp.float32
BF16 = jnp.bfloat16


def flip(index, bits):
    out, bit = index, 1
    while bit <= bits:
        if bits & bit:
            out = out + bit * (1 - 2 * lax.rem(lax.div(index, bit), 2))
        bit *= 2
    return out


def interleaved(count):
    far, near = list(range(count // 2, count)), list(range(1, count // 2))
    order = []
    for k in range(len(far)):
        order.append(far[k])
        if k < len(near):
            order.append(near[k])
    return order


def dot(a, b, precision=None):
    return jnp.dot(a, b, precision=precision, preferred_element_type=F32)


def dot_nt(a, b):
    return lax.dot_general(a, b, (((1,), (1,)), ((), ())), preferred_element_type=F32)


def dot_tn(a, b):
    return lax.dot_general(a, b, (((0,), (0,)), ((), ())), preferred_element_type=F32)


def kernel(
    dims,
    first_hbm, second_hbm, third_hbm, heads_hbm, residue_hbm, decay_hbm, skip_hbm,
    first, second, stage_third, conv, leave_buf, fall_wide, out_residue, out_skip,
    third, heads, x_buf, g_buf, cross_buf,
    toep, enter_buf, fwd_pow, bwd_pow, fwd_slots, bwd_slots, sum_slots,
    residue_ref, decay_ref, skip_ref,
    load_sem, send_sem, recv_sem, fwd_send, fwd_recv, bwd_send, bwd_recv, sum_send, sum_recv,
):
    nch, nctx, channels, length, groups, modes, seq_total = dims
    width = channels // groups
    chunk = length // nch
    span = min(256, length)
    spans = length // span
    lanes = groups * modes
    unit = max(chunk, span)
    per_unit = unit // chunk
    unit_spans = unit // span
    units = length // unit
    batches = 4 if units % 4 == 0 else 1
    batch_units = units // batches
    batch_spans = spans // batches
    me = lax.axis_index("ch")
    me_x = lax.axis_index("ctx")

    loads = [
        pltpu.make_async_copy(src, dst, load_sem.at[k])
        for k, (src, dst) in enumerate(
            (
                (first_hbm, first),
                (second_hbm, second),
                (third_hbm, third),
                (residue_hbm, residue_ref),
                (decay_hbm, decay_ref),
                (skip_hbm, skip_ref),
            )
        )
    ]
    for k in (4, 3, 5, 0, 1):
        loads[k].start()

    def rows_of(index):
        return pl.ds(pl.multiple_of(index * channels, channels), channels)

    def cols_of(index):
        return pl.ds(pl.multiple_of(index * chunk, chunk), chunk)

    own = pltpu.make_async_copy(
        heads_hbm.at[rows_of(me)], heads.at[:, cols_of(me)], recv_sem.at[me]
    )

    barrier = pltpu.get_barrier_semaphore()
    for s in range(1, nch):
        pl.semaphore_signal(barrier, inc=1, device_id={"ch": flip(me, s)}, device_id_type=MESH)
    for k in range(1, nctx):
        pl.semaphore_signal(
            barrier, inc=1, device_id={"ctx": lax.rem(me_x + k, nctx)}, device_id_type=MESH
        )
    pl.semaphore_wait(barrier, nch - 1 + nctx - 1)

    sends = []
    for s in interleaved(nch):
        to = flip(me, s)
        copy = pltpu.make_async_remote_copy(
            src_ref=heads_hbm.at[rows_of(to)],
            dst_ref=heads.at[:, cols_of(me)],
            send_sem=send_sem.at[s],
            recv_sem=recv_sem.at[me],
            device_id={"ch": to},
            device_id_type=MESH,
        )
        copy.start()
        sends.append(copy)
    own.start()
    loads[2].start()

    def spread(slots, send, recv):
        copies = []
        for k in range(1, nctx):
            copy = pltpu.make_async_remote_copy(
                src_ref=slots.at[me_x],
                dst_ref=slots.at[me_x],
                send_sem=send.at[k],
                recv_sem=recv.at[me_x],
                device_id={"ctx": lax.rem(me_x + k, nctx)},
                device_id_type=MESH,
            )
            copy.start()
            copies.append(copy)
        return copies

    def gather(slots, send, recv):
        for k in range(1, nctx):
            at = lax.rem(me_x + k, nctx)
            pltpu.make_async_remote_copy(
                src_ref=slots.at[at],
                dst_ref=slots.at[at],
                send_sem=send.at[k],
                recv_sem=recv.at[at],
                device_id={"ctx": at},
                device_id_type=MESH,
            ).wait_recv()

    def iota(shape, dim):
        return lax.broadcasted_iota(jnp.int32, shape, dim)

    def column(row):
        size = row.shape[1]
        eye = iota((size, size), 0) == iota((size, size), 1)
        return jnp.sum(jnp.where(eye, jnp.broadcast_to(row, (size, size)), 0.0), axis=1, keepdims=True)

    for k in (4, 3, 5):
        loads[k].wait()
    middle = float(span // 2)
    rate = jnp.concatenate([decay_ref[g : g + 1, :] for g in range(groups)], axis=1)
    weight = jnp.concatenate([residue_ref[g : g + 1, :] for g in range(groups)], axis=1)
    root = jnp.sqrt(2.0 * rate)
    weight = weight * root
    rate_c, weight_c = column(rate), column(weight)
    from_middle = iota((lanes, span), 1).astype(F32) - middle
    falling = weight_c * jnp.exp(-rate_c * from_middle)
    rising = jnp.exp(rate_c * from_middle)
    row_group = lax.div(iota((lanes, span), 0), modes)
    lane_group = lax.div(iota((span, lanes), 1), modes)

    def wide(table):
        return jnp.concatenate(
            [jnp.where(row_group == g, table, 0.0) for g in range(groups)], axis=1
        ).astype(BF16)

    def tall(table):
        return jnp.concatenate(
            [jnp.where(lane_group == g, table, 0.0) for g in range(groups)], axis=0
        ).astype(BF16)

    def split(table):
        high = table.astype(BF16)
        return high, (table - high.astype(F32)).astype(BF16)

    rise_wide = wide(falling * jnp.exp(-rate_c * middle))
    fall_wide[...] = wide(weight_c * rising * jnp.exp(-rate_c * (span - 1.0 - middle)))
    from_middle_col = iota((span, lanes), 0).astype(F32) - middle
    fall_col = jnp.exp(-rate * from_middle_col)
    rise_col = jnp.exp(rate * from_middle_col)
    tail = tall(rise_col * jnp.exp(-rate * (span - middle)))
    decay_in = tall(fall_col * jnp.exp(-rate * middle))
    rise_col = rise_col.astype(BF16)

    loads[0].wait()
    loads[1].wait()

    def gate(n, carry):
        at = pl.ds(pl.multiple_of(n * span, span), span)
        gated = (first[:, at].astype(F32) * second[:, at].astype(F32)).astype(BF16)
        rows = pl.ds(pl.multiple_of(n * width, width), width)
        for g in range(groups):
            x_buf[rows, g * span : (g + 1) * span] = gated[g * width : (g + 1) * width]
        return carry

    lax.fori_loop(0, spans, gate, 0, unroll=8)

    state = dot(x_buf[...], tail)
    span_decay = jnp.exp(-rate * span)
    powers = jnp.exp(-rate * span * iota((spans, lanes), 0).astype(F32))
    run = jnp.zeros((width, lanes), F32)
    for n in range(spans):
        at = slice(n * width, (n + 1) * width)
        enter_buf[at, :] = run
        run = run * span_decay + state[at]
    fwd_slots[me_x] = run
    fwd_copies = spread(fwd_slots, fwd_send, fwd_recv)

    lower = iota((span, span), 0) >= iota((span, span), 1)
    fall_high, fall_low = split(falling)
    rise_high, rise_low = split(rising)
    for g in range(groups):
        at = slice(g * modes, (g + 1) * modes)
        toeplitz = dot_tn(
            jnp.concatenate([fall_high[at], fall_high[at], fall_low[at]], axis=0),
            jnp.concatenate([rise_high[at], rise_low[at], rise_high[at]], axis=0),
        )
        toep[g] = jnp.where(lower, toeplitz, 0.0).astype(BF16)
        at = slice(g * span, (g + 1) * span)
        conv[:, at] = dot_nt(x_buf[:, at], toep[g])
    for n in range(spans):
        power = jnp.broadcast_to(powers[n : n + 1], (width, lanes))
        fwd_pow[n * width : (n + 1) * width, :] = power
        bwd_pow[(spans - 1 - n) * width : (spans - n) * width, :] = power
    skip_wide = jnp.broadcast_to(column(skip_ref[...]), (channels, span))
    gather(fwd_slots, fwd_send, fwd_recv)

    def entering(slots, before):
        total = jnp.zeros((width, lanes), F32)
        for k in range(nctx):
            gap = me_x - 1 - k if before else k - 1 - me_x
            steps = jnp.maximum(gap, 0).astype(F32)
            decayed = slots[k] * jnp.exp(-rate * length * steps)
            total = total + jnp.where(gap >= 0, decayed, 0.0)
        return jnp.concatenate([total] * spans, axis=0)

    enter = enter_buf[...] + fwd_pow[...] * entering(fwd_slots, True)
    enter_buf[...] = enter
    conv[...] = conv[...] + dot(enter.astype(BF16), rise_wide)

    loads[2].wait()
    batch_rows = batch_spans * width
    skip_sum = jnp.zeros((channels, span), F32)
    far_sum = jnp.zeros((batch_rows, lanes), F32)
    bwd_sum = jnp.zeros((batch_rows, lanes), F32)
    bwd_copies = []
    state_decay = jnp.exp(-rate)
    for k in range(batches):
        for p in range(batch_units):
            at_unit = flip(lax.div(me, per_unit), k * batch_units + p)
            for q in range(per_unit):
                src = at_unit * per_unit + q
                pltpu.make_async_copy(
                    heads_hbm.at[rows_of(0)], heads.at[:, cols_of(src)], recv_sem.at[src]
                ).wait()
            for q in range(unit_spans):
                n = at_unit * unit_spans + q
                cols = pl.ds(pl.multiple_of(n * span, span), span)
                rows = pl.ds(pl.multiple_of(n * width, width), width)

                def stacked(ref):
                    return jnp.concatenate(
                        [ref[rows, g * span : (g + 1) * span] for g in range(groups)], axis=0
                    ).astype(F32)

                out_grad = heads[:, cols].astype(F32)
                grad = out_grad * third[:, cols].astype(F32)
                gated = stacked(x_buf)
                skip_sum = skip_sum + grad * gated
                convolved = stacked(conv) + skip_wide * gated
                stage_third[:, cols] = (out_grad * convolved).astype(BF16)
                rounded, direct = grad.astype(BF16), skip_wide * grad
                for g in range(groups):
                    at = slice(g * width, (g + 1) * width)
                    g_buf[rows, g * span : (g + 1) * span] = rounded[at]
                    conv[rows, g * span : (g + 1) * span] = direct[at]
        at_batch = flip(lax.div(me, nch // batches), k)
        rows = pl.ds(pl.multiple_of(at_batch * batch_rows, batch_rows), batch_rows)
        weighted = dot(g_buf[rows, :], decay_in)
        state = weighted * state_decay
        bwd_sum = bwd_sum + state * fwd_pow[rows, :]
        if k == batches - 1:
            run = bwd_sum[0:width]
            for q in range(1, batch_spans):
                run = run + bwd_sum[q * width : (q + 1) * width]
            bwd_slots[me_x] = run
            bwd_copies = spread(bwd_slots, bwd_send, bwd_recv)
        leave_buf[rows, :] = state
        far_sum = far_sum + weighted * enter_buf[rows, :]
        for g in range(groups):
            at = slice(g * span, (g + 1) * span)
            part = g_buf[rows, at]
            conv[rows, at] = conv[rows, at] + dot(part, toep[g])
            cross = dot_tn(part, x_buf[rows, at])
            cross_buf[g] = cross if k == 0 else cross_buf[g] + cross

    filter_sum = jnp.sum(far_sum, axis=0, keepdims=True)
    for g in range(groups):
        cross = jnp.where(lower, cross_buf[g], 0.0).astype(BF16)
        near = jnp.sum(dot(cross, rise_col) * fall_col, axis=0, keepdims=True)
        filter_sum = filter_sum + jnp.where(lane_group[0:1] == g, near, 0.0)
    skip_total = jnp.sum(skip_sum, axis=1, keepdims=True)
    eye = iota((channels, channels), 0) == iota((channels, channels), 1)
    sum_slots[me_x] = jnp.zeros(sum_slots.shape[1:], F32)
    sum_slots[me_x, 0:1, 0:lanes] = root * filter_sum
    sum_slots[me_x, 1:2, 0:channels] = jnp.sum(
        jnp.where(eye, jnp.broadcast_to(skip_total, (channels, channels)), 0.0),
        axis=0,
        keepdims=True,
    )
    sum_copies = spread(sum_slots, sum_send, sum_recv)
    run = jnp.zeros((width, lanes), F32)
    for n in reversed(range(spans)):
        at = slice(n * width, (n + 1) * width)
        state = leave_buf[at, :]
        leave_buf[at, :] = run
        run = run * span_decay + state

    gather(bwd_slots, bwd_send, bwd_recv)
    leave_buf[...] = leave_buf[...] + bwd_pow[...] * entering(bwd_slots, False)

    gather(sum_slots, sum_send, sum_recv)
    total = sum_slots[0]
    for k in range(1, nctx):
        total = total + sum_slots[k]
    for g in range(groups):
        out_residue[g : g + 1, :] = total[0:1, g * modes : (g + 1) * modes] / jnp.sqrt(
            F32(width * seq_total)
        )
    out_skip[...] = total[1:2, 0:channels] / jnp.sqrt(F32(seq_total))

    for copy in sends + fwd_copies + bwd_copies + sum_copies:
        copy.wait_send()


def finish(
    width,
    first, second, third, conv, leave, fall_wide, residue, skip,
    out_first, out_second, out_third, out_residue, out_skip,
    stage_first, stage_second, sem,
):
    channels, length = first.shape
    groups = channels // width
    span = conv.shape[1] // groups
    spans = length // span
    pieces = 4 if spans % 4 == 0 else 1
    piece_spans = spans // pieces
    copies = []

    def send(src, dst):
        copies.append(pltpu.make_async_copy(src, dst, sem.at[len(copies)]))
        copies[-1].start()

    for p in range(pieces):
        cols = pl.ds(p * piece_spans * span, piece_spans * span)
        send(third.at[:, cols], out_third.at[:, cols])
    send(residue, out_residue)
    send(skip, out_skip)
    for p in range(pieces):
        rows = slice(p * piece_spans * width, (p + 1) * piece_spans * width)
        for g in range(groups):
            lanes = slice(g * span, (g + 1) * span)
            mixed = conv[rows, lanes] + dot(leave[rows, :].astype(BF16), fall_wide[:, lanes])
            for q in range(piece_spans):
                n = p * piece_spans + q
                part = mixed[q * width : (q + 1) * width]
                at = (slice(g * width, (g + 1) * width), slice(n * span, (n + 1) * span))
                stage_first[at] = (part * second[at].astype(F32)).astype(BF16)
                stage_second[at] = (part * first[at].astype(F32)).astype(BF16)
        cols = pl.ds(p * piece_spans * span, piece_spans * span)
        send(stage_first.at[:, cols], out_first.at[:, cols])
        send(stage_second.at[:, cols], out_second.at[:, cols])
    for copy in copies:
        copy.wait()


def on_device(nch, nctx, first_in, second_in, third_in, grad_heads, residue, decay_rate, skip_gain):
    channels, length = first_in.shape
    groups, modes = residue.shape
    width = channels // groups
    span = min(256, length)
    rows = length // span * width
    lanes = groups * modes
    dims = (nch, nctx, channels, length, groups, modes, length * nctx)
    whole, vmem = pl.BlockSpec(memory_space=pltpu.HBM), pl.BlockSpec(memory_space=pltpu.VMEM)
    big = jax.ShapeDtypeStruct((channels, length), BF16)
    small = (
        jax.ShapeDtypeStruct((groups, modes), F32),
        jax.ShapeDtypeStruct((1, channels), F32),
    )
    big_buf = pltpu.VMEM((channels, length), BF16)
    half_buf = pltpu.VMEM((rows, groups * span), BF16)
    state_buf = pltpu.VMEM((rows, lanes), F32)
    slots = pltpu.VMEM((nctx, width, lanes), F32)
    dma = pltpu.SemaphoreType.DMA
    outs = pl.pallas_call(
        functools.partial(kernel, dims),
        out_shape=(
            big, big, big,
            jax.ShapeDtypeStruct((rows, groups * span), F32),
            jax.ShapeDtypeStruct((rows, lanes), F32),
            jax.ShapeDtypeStruct((lanes, groups * span), BF16),
            *small,
        ),
        in_specs=[whole] * 7,
        out_specs=[vmem] * 8,
        scratch_shapes=[
            big_buf, big_buf,
            half_buf, half_buf,
            pltpu.VMEM((groups, span, span), F32),
            pltpu.VMEM((groups, span, span), BF16),
            state_buf, state_buf, state_buf,
            slots, slots,
            pltpu.VMEM((nctx, 8, 128), F32),
            pltpu.VMEM((groups, modes), F32),
            pltpu.VMEM((groups, modes), F32),
            pltpu.VMEM((1, channels), F32),
            dma((6,)),
            dma((nch,)), dma((nch,)),
            dma((nctx,)), dma((nctx,)), dma((nctx,)), dma((nctx,)), dma((nctx,)), dma((nctx,)),
        ],
        compiler_params=pltpu.CompilerParams(
            collective_id=0, has_side_effects=True, vmem_limit_bytes=32 * 1024 * 1024
        ),
        cost_estimate=pl.CostEstimate(
            flops=12 * channels * length * span, bytes_accessed=14 * channels * length,
            transcendentals=0,
        ),
    )(
        *(
            pltpu.with_memory_space_constraint(part, pltpu.HBM)
            for part in (
                first_in, second_in, third_in, grad_heads, residue, decay_rate,
                skip_gain.reshape(1, channels),
            )
        )
    )
    outs = pl.pallas_call(
        functools.partial(finish, width),
        out_shape=(big, big, big, *small),
        in_specs=[vmem] * 8,
        out_specs=[whole] * 5,
        scratch_shapes=[big_buf, big_buf, dma((14,))],
        compiler_params=pltpu.CompilerParams(vmem_limit_bytes=16 * 1024 * 1024),
    )(*outs)
    return (*outs[:4], outs[4].reshape(channels))


def solution(mesh):
    return jax.shard_map(
        functools.partial(on_device, mesh.shape["ch"], mesh.shape["ctx"]),
        mesh=mesh,
        in_specs=(
            P("ch", "ctx"),
            P("ch", "ctx"),
            P("ch", "ctx"),
            P(None, ("ctx", "ch")),
            P("ch", None),
            P("ch", None),
            P("ch"),
        ),
        out_specs=(P("ch", "ctx"), P("ch", "ctx"), P("ch", "ctx"), P("ch", None), P("ch")),
        check_vma=False,
    )
```

time: 22.9 us -> 22.9 us (level)
  no operation moved by 1% of the time
where the time goes in v3:
time: 22.9 us; the launch traced here: 22.7 us
  Pallas kernels  22.1 us (97%)
  between operations  0.64 us (3%)
    pallas_call x1, Pallas kernels, on_device(): pl.pallas_call(functools.partial(kernel, dims), out_shape=(big, big, big,...  20.8 us
    pallas_call x1, Pallas kernels, on_device(): pl.pallas_call(functools.partial(finish, width), out_shape=(big, big, big...  1.27 us

profile of v3, /device:TPU:8, one launch (start us, length us, event | category | flops | bytes accessed | tf_op | source)
XLA Modules:
  0.0 22.7 jit_solution(18432676111350505954)
XLA Ops:
  0.6 20.8 %shard_map.110 = (bf16[32,8192]{1,0:T(8,128)(2,1)S(1)}, bf16[32,8192]{1,0:T(8,128)(2,1)S(1)}, bf16[32,8192]{1,0:T(8,128)(2,1)S(1)}, f32[512,512]{1,0:T(8,128)S(1...) custom-call(bf16[32,8192]{1,0:T(8,128)(2,1)} %first_hbm.1, ...), custom_call_target="tpu_custom_call" | custom-call | flops 805306368 | bytes 3670016 | tf_op jit(solution)/shard_map/pallas_call | solution.py:406
  21.4 1.3 %shard_map.111 = (bf16[32,8192]{1,0:T(8,128)(2,1)}, bf16[32,8192]{1,0:T(8,128)(2,1)}, bf16[32,8192]{1,0:T(8,128)(2,1)}, f32[2,16]{1,0:T(2,128)}, f32[1,32]{1,0:T(1,128)}) custom-call(bf16[32,8192]{1,0:T(8,128)(2,1)S(1)} %get-tuple-element.18.first, bf16[32,8192]{1,0:T(8,128)(2,1)S(1)} %get-tuple-element.19.second, ...), custom_call_target="tpu_custom_call" | custom-call | tf_op jit(solution)/shard_map/pallas_call | solution.py:448

commit v4 on v3

--- a/solution.py
+++ b/solution.py
@@ -22,14 +22,9 @@
     return out
 
 
-def interleaved(count):
-    far, near = list(range(count // 2, count)), list(range(1, count // 2))
-    order = []
-    for k in range(len(far)):
-        order.append(far[k])
-        if k < len(near):
-            order.append(near[k])
-    return order
+def far_first(count):
+    half, quarter = count // 2, max(count // 4, 1)
+    return [*range(half, count), *range(quarter, half), *range(1, quarter)]
 
 
 def dot(a, b, precision=None):
@@ -105,7 +100,7 @@
     pl.semaphore_wait(barrier, nch - 1 + nctx - 1)
 
     sends = []
-    for s in interleaved(nch):
+    for s in far_first(nch):
         to = flip(me, s)
         copy = pltpu.make_async_remote_copy(
             src_ref=heads_hbm.at[rows_of(to)],

time: 22.9 us -> 22.9 us (level)
  no operation moved by 1% of the time
where the time goes in v4:
time: 22.9 us; the launch traced here: 22.7 us
  Pallas kernels  22.1 us (97%)
  between operations  0.64 us (3%)
    pallas_call x1, Pallas kernels, on_device(): pl.pallas_call(functools.partial(kernel, dims), out_shape=(big, big, big,...  20.8 us
    pallas_call x1, Pallas kernels, on_device(): pl.pallas_call(functools.partial(finish, width), out_shape=(big, big, big...  1.27 us

profile of v4, /device:TPU:8, one launch (start us, length us, event | category | flops | bytes accessed | tf_op | source)
XLA Modules:
  0.0 22.7 jit_solution(8549502944755239797)
XLA Ops:
  0.6 20.8 %shard_map.110 = (bf16[32,8192]{1,0:T(8,128)(2,1)S(1)}, bf16[32,8192]{1,0:T(8,128)(2,1)S(1)}, bf16[32,8192]{1,0:T(8,128)(2,1)S(1)}, f32[512,512]{1,0:T(8,128)S(1...) custom-call(bf16[32,8192]{1,0:T(8,128)(2,1)} %first_hbm.1, ...), custom_call_target="tpu_custom_call" | custom-call | flops 805306368 | bytes 3670016 | tf_op jit(solution)/shard_map/pallas_call | solution.py:401
  21.4 1.3 %shard_map.111 = (bf16[32,8192]{1,0:T(8,128)(2,1)}, bf16[32,8192]{1,0:T(8,128)(2,1)}, bf16[32,8192]{1,0:T(8,128)(2,1)}, f32[2,16]{1,0:T(2,128)}, f32[1,32]{1,0:T(1,128)}) custom-call(bf16[32,8192]{1,0:T(8,128)(2,1)S(1)} %get-tuple-element.18.first, bf16[32,8192]{1,0:T(8,128)(2,1)S(1)} %get-tuple-element.19.second, ...), custom_call_target="tpu_custom_call" | custom-call | tf_op jit(solution)/shard_map/pallas_call | solution.py:443

commit v5 on v4

--- a/solution.py
+++ b/solution.py
@@ -20,11 +20,6 @@
             out = out + bit * (1 - 2 * lax.rem(lax.div(index, bit), 2))
         bit *= 2
     return out
-
-
-def far_first(count):
-    half, quarter = count // 2, max(count // 4, 1)
-    return [*range(half, count), *range(quarter, half), *range(1, quarter)]
 
 
 def dot(a, b, precision=None):
@@ -58,9 +53,9 @@
     per_unit = unit // chunk
     unit_spans = unit // span
     units = length // unit
-    batches = 4 if units % 4 == 0 else 1
-    batch_units = units // batches
-    batch_spans = spans // batches
+    batches = [(units, 0)]
+    if units % 8 == 0:
+        batches = [(units // 4, k) for k in range(3)] + [(units // 8, 6), (units // 8, 7)]
     me = lax.axis_index("ch")
     me_x = lax.axis_index("ctx")
 
@@ -77,9 +72,6 @@
             )
         )
     ]
-    for k in (4, 3, 5, 0, 1):
-        loads[k].start()
-
     def rows_of(index):
         return pl.ds(pl.multiple_of(index * channels, channels), channels)
 
@@ -97,21 +89,29 @@
         pl.semaphore_signal(
             barrier, inc=1, device_id={"ctx": lax.rem(me_x + k, nctx)}, device_id_type=MESH
         )
+    for k in (4, 3, 5, 0, 1):
+        loads[k].start()
     pl.semaphore_wait(barrier, nch - 1 + nctx - 1)
 
     sends = []
-    for s in far_first(nch):
-        to = flip(me, s)
-        copy = pltpu.make_async_remote_copy(
-            src_ref=heads_hbm.at[rows_of(to)],
-            dst_ref=heads.at[:, cols_of(me)],
-            send_sem=send_sem.at[s],
-            recv_sem=recv_sem.at[me],
-            device_id={"ch": to},
-            device_id_type=MESH,
-        )
-        copy.start()
-        sends.append(copy)
+
+    def send_to(places):
+        for s in places:
+            to = flip(me, s)
+            copy = pltpu.make_async_remote_copy(
+                src_ref=heads_hbm.at[rows_of(to)],
+                dst_ref=heads.at[:, cols_of(me)],
+                send_sem=send_sem.at[s],
+                recv_sem=recv_sem.at[me],
+                device_id={"ch": to},
+                device_id_type=MESH,
+            )
+            copy.start()
+            sends.append(copy)
+
+    first_step, second_step = nch * 3 // 4, nch * 7 // 8
+    send_to(range(nch // 2, first_step))
+    send_to(range(1, nch // 2))
     own.start()
     loads[2].start()
 
@@ -243,21 +243,31 @@
     enter_buf[...] = enter
     conv[...] = conv[...] + dot(enter.astype(BF16), rise_wide)
 
+    send_to(range(first_step, second_step))
+
     loads[2].wait()
-    batch_rows = batch_spans * width
     skip_sum = jnp.zeros((channels, span), F32)
-    far_sum = jnp.zeros((batch_rows, lanes), F32)
-    bwd_sum = jnp.zeros((batch_rows, lanes), F32)
+    far_sum = jnp.zeros((width, lanes), F32)
+    bwd_sum = jnp.zeros((width, lanes), F32)
+
+    def over_spans(rows):
+        total = rows[0:width]
+        for at in range(width, rows.shape[0], width):
+            total = total + rows[at : at + width]
+        return total
+
     bwd_copies = []
     state_decay = jnp.exp(-rate)
-    for k in range(batches):
+    for k, (batch_units, place) in enumerate(batches):
         for p in range(batch_units):
-            at_unit = flip(lax.div(me, per_unit), k * batch_units + p)
+            at_unit = flip(lax.div(me, per_unit), place * batch_units + p)
             for q in range(per_unit):
                 src = at_unit * per_unit + q
                 pltpu.make_async_copy(
                     heads_hbm.at[rows_of(0)], heads.at[:, cols_of(src)], recv_sem.at[src]
                 ).wait()
+            if p == 0 and k == min(2, len(batches) - 1):
+                send_to(range(second_step, nch))
             for q in range(unit_spans):
                 n = at_unit * unit_spans + q
                 cols = pl.ds(pl.multiple_of(n * span, span), span)
@@ -279,25 +289,24 @@
                     at = slice(g * width, (g + 1) * width)
                     g_buf[rows, g * span : (g + 1) * span] = rounded[at]
                     conv[rows, g * span : (g + 1) * span] = direct[at]
-        at_batch = flip(lax.div(me, nch // batches), k)
+        at_batch = flip(lax.div(me, per_unit * batch_units), place)
+        batch_rows = batch_units * unit_spans * width
         rows = pl.ds(pl.multiple_of(at_batch * batch_rows, batch_rows), batch_rows)
         weighted = dot(g_buf[rows, :], decay_in)
         state = weighted * state_decay
-        bwd_sum = bwd_sum + state * fwd_pow[rows, :]
-        if k == batches - 1:
-            run = bwd_sum[0:width]
-            for q in range(1, batch_spans):
-                run = run + bwd_sum[q * width : (q + 1) * width]
-            bwd_slots[me_x] = run
+        bwd_sum = bwd_sum + over_spans(state * fwd_pow[rows, :])
+        if k == len(batches) - 1:
+            bwd_slots[me_x] = bwd_sum
             bwd_copies = spread(bwd_slots, bwd_send, bwd_recv)
         leave_buf[rows, :] = state
-        far_sum = far_sum + weighted * enter_buf[rows, :]
+        far_sum = far_sum + over_spans(weighted * enter_buf[rows, :])
         for g in range(groups):
             at = slice(g * span, (g + 1) * span)
             part = g_buf[rows, at]
-            conv[rows, at] = conv[rows, at] + dot(part, toep[g])
             cross = dot_tn(part, x_buf[rows, at])
             cross_buf[g] = cross if k == 0 else cross_buf[g] + cross
+            if k < len(batches) - 1:
+                conv[rows, at] = conv[rows, at] + dot(part, toep[g])
 
     filter_sum = jnp.sum(far_sum, axis=0, keepdims=True)
     for g in range(groups):
@@ -314,6 +323,9 @@
         keepdims=True,
     )
     sum_copies = spread(sum_slots, sum_send, sum_recv)
+    for g in range(groups):
+        at = slice(g * span, (g + 1) * span)
+        conv[rows, at] = conv[rows, at] + dot(g_buf[rows, at], toep[g])
     run = jnp.zeros((width, lanes), F32)
     for n in reversed(range(spans)):
         at = slice(n * width, (n + 1) * width)

time: 22.9 us -> 22.9 us (level)
  no operation moved by 1% of the time
where the time goes in v5:
time: 22.9 us; the launch traced here: 22.7 us
  Pallas kernels  22.1 us (97%)
  between operations  0.64 us (3%)
    pallas_call x1, Pallas kernels, on_device(): pl.pallas_call(functools.partial(kernel, dims), out_shape=(big, big, big,...  20.8 us
    pallas_call x1, Pallas kernels, on_device(): pl.pallas_call(functools.partial(finish, width), out_shape=(big, big, big...  1.27 us

profile of v5, /device:TPU:8, one launch (start us, length us, event | category | flops | bytes accessed | tf_op | source)
XLA Modules:
  0.0 22.7 jit_solution(5571180776552713088)
XLA Ops:
  0.6 20.8 %shard_map.110 = (bf16[32,8192]{1,0:T(8,128)(2,1)S(1)}, bf16[32,8192]{1,0:T(8,128)(2,1)S(1)}, bf16[32,8192]{1,0:T(8,128)(2,1)S(1)}, f32[512,512]{1,0:T(8,128)S(1...) custom-call(bf16[32,8192]{1,0:T(8,128)(2,1)} %first_hbm.1, ...), custom_call_target="tpu_custom_call" | custom-call | flops 805306368 | bytes 3670016 | tf_op jit(solution)/shard_map/pallas_call | solution.py:413
  21.4 1.3 %shard_map.111 = (bf16[32,8192]{1,0:T(8,128)(2,1)}, bf16[32,8192]{1,0:T(8,128)(2,1)}, bf16[32,8192]{1,0:T(8,128)(2,1)}, f32[2,16]{1,0:T(2,128)}, f32[1,32]{1,0:T(1,128)}) custom-call(bf16[32,8192]{1,0:T(8,128)(2,1)S(1)} %get-tuple-element.18.first, bf16[32,8192]{1,0:T(8,128)(2,1)S(1)} %get-tuple-element.19.second, ...), custom_call_target="tpu_custom_call" | custom-call | tf_op jit(solution)/shard_map/pallas_call | solution.py:455

commit v6 on v5

--- a/solution.py
+++ b/solution.py
@@ -75,11 +75,8 @@
     def rows_of(index):
         return pl.ds(pl.multiple_of(index * channels, channels), channels)
 
-    def cols_of(index):
-        return pl.ds(pl.multiple_of(index * chunk, chunk), chunk)
-
     own = pltpu.make_async_copy(
-        heads_hbm.at[rows_of(me)], heads.at[:, cols_of(me)], recv_sem.at[me]
+        heads_hbm.at[rows_of(me)], heads.at[me], recv_sem.at[me]
     )
 
     barrier = pltpu.get_barrier_semaphore()
@@ -100,7 +97,7 @@
             to = flip(me, s)
             copy = pltpu.make_async_remote_copy(
                 src_ref=heads_hbm.at[rows_of(to)],
-                dst_ref=heads.at[:, cols_of(me)],
+                dst_ref=heads.at[me],
                 send_sem=send_sem.at[s],
                 recv_sem=recv_sem.at[me],
                 device_id={"ch": to},
@@ -109,8 +106,7 @@
             copy.start()
             sends.append(copy)
 
-    first_step, second_step = nch * 3 // 4, nch * 7 // 8
-    send_to(range(nch // 2, first_step))
+    send_to(range(nch // 2, nch * 3 // 4))
     send_to(range(1, nch // 2))
     own.start()
     loads[2].start()
@@ -243,7 +239,7 @@
     enter_buf[...] = enter
     conv[...] = conv[...] + dot(enter.astype(BF16), rise_wide)
 
-    send_to(range(first_step, second_step))
+    send_to(range(nch * 3 // 4, nch))
 
     loads[2].wait()
     skip_sum = jnp.zeros((channels, span), F32)
@@ -264,10 +260,8 @@
             for q in range(per_unit):
                 src = at_unit * per_unit + q
                 pltpu.make_async_copy(
-                    heads_hbm.at[rows_of(0)], heads.at[:, cols_of(src)], recv_sem.at[src]
+                    heads_hbm.at[rows_of(0)], heads.at[src], recv_sem.at[src]
                 ).wait()
-            if p == 0 and k == min(2, len(batches) - 1):
-                send_to(range(second_step, nch))
             for q in range(unit_spans):
                 n = at_unit * unit_spans + q
                 cols = pl.ds(pl.multiple_of(n * span, span), span)
@@ -278,7 +272,12 @@
                         [ref[rows, g * span : (g + 1) * span] for g in range(groups)], axis=0
                     ).astype(F32)
 
-                out_grad = heads[:, cols].astype(F32)
+                if chunk >= span:
+                    out_grad = heads[at_unit, :, q * span : (q + 1) * span].astype(F32)
+                else:
+                    out_grad = jnp.concatenate(
+                        [heads[at_unit * per_unit + j] for j in range(per_unit)], axis=1
+                    ).astype(F32)
                 grad = out_grad * third[:, cols].astype(F32)
                 gated = stacked(x_buf)
                 skip_sum = skip_sum + grad * gated
@@ -422,7 +421,7 @@
         in_specs=[whole] * 7,
         out_specs=[vmem] * 8,
         scratch_shapes=[
-            big_buf, big_buf,
+            big_buf, pltpu.VMEM((nch, channels, length // nch), BF16),
             half_buf, half_buf,
             pltpu.VMEM((groups, span, span), F32),
             pltpu.VMEM((groups, span, span), BF16),

time: 22.9 us -> 22.9 us (level)
  no operation moved by 1% of the time
where the time goes in v6:
time: 22.9 us; the launch traced here: 22.7 us
  Pallas kernels  22.1 us (97%)
  between operations  0.64 us (3%)
    pallas_call x1, Pallas kernels, on_device(): pl.pallas_call(functools.partial(kernel, dims), out_shape=(big, big, big,...  20.8 us
    pallas_call x1, Pallas kernels, on_device(): pl.pallas_call(functools.partial(finish, width), out_shape=(big, big, big...  1.27 us

profile of v6, /device:TPU:8, one launch (start us, length us, event | category | flops | bytes accessed | tf_op | source)
XLA Modules:
  0.0 22.7 jit_solution(193608604138092339)
XLA Ops:
  0.6 20.8 %shard_map.110 = (bf16[32,8192]{1,0:T(8,128)(2,1)S(1)}, bf16[32,8192]{1,0:T(8,128)(2,1)S(1)}, bf16[32,8192]{1,0:T(8,128)(2,1)S(1)}, f32[512,512]{1,0:T(8,128)S(1...) custom-call(bf16[32,8192]{1,0:T(8,128)(2,1)} %first_hbm.1, ...), custom_call_target="tpu_custom_call" | custom-call | flops 805306368 | bytes 3670016 | tf_op jit(solution)/shard_map/pallas_call | solution.py:412
  21.4 1.3 %shard_map.111 = (bf16[32,8192]{1,0:T(8,128)(2,1)}, bf16[32,8192]{1,0:T(8,128)(2,1)}, bf16[32,8192]{1,0:T(8,128)(2,1)}, f32[2,16]{1,0:T(2,128)}, f32[1,32]{1,0:T(1,128)}) custom-call(bf16[32,8192]{1,0:T(8,128)(2,1)S(1)} %get-tuple-element.18.first, bf16[32,8192]{1,0:T(8,128)(2,1)S(1)} %get-tuple-element.19.second, ...), custom_call_target="tpu_custom_call" | custom-call | tf_op jit(solution)/shard_map/pallas_call | solution.py:454

commit v7 on v6

--- a/solution.py
+++ b/solution.py
@@ -22,6 +22,16 @@
     return out
 
 
+def interleaved(count):
+    far, near = list(range(count // 2, count)), list(range(1, count // 2))
+    order = []
+    for k in range(len(far)):
+        order.append(far[k])
+        if k < len(near):
+            order.append(near[k])
+    return order
+
+
 def dot(a, b, precision=None):
     return jnp.dot(a, b, precision=precision, preferred_element_type=F32)
 
@@ -39,7 +49,7 @@
     first_hbm, second_hbm, third_hbm, heads_hbm, residue_hbm, decay_hbm, skip_hbm,
     first, second, stage_third, conv, leave_buf, fall_wide, out_residue, out_skip,
     third, heads, x_buf, g_buf, cross_buf,
-    toep, enter_buf, fwd_pow, bwd_pow, fwd_slots, bwd_slots, sum_slots,
+    toep, toep_low, enter_buf, fwd_pow, bwd_pow, fwd_slots, bwd_slots, sum_slots,
     residue_ref, decay_ref, skip_ref,
     load_sem, send_sem, recv_sem, fwd_send, fwd_recv, bwd_send, bwd_recv, sum_send, sum_recv,
 ):
@@ -106,8 +116,7 @@
             copy.start()
             sends.append(copy)
 
-    send_to(range(nch // 2, nch * 3 // 4))
-    send_to(range(1, nch // 2))
+    send_to(interleaved(nch))
     own.start()
     loads[2].start()
 
@@ -163,24 +172,24 @@
     def wide(table):
         return jnp.concatenate(
             [jnp.where(row_group == g, table, 0.0) for g in range(groups)], axis=1
-        ).astype(BF16)
+        )
 
     def tall(table):
         return jnp.concatenate(
             [jnp.where(lane_group == g, table, 0.0) for g in range(groups)], axis=0
-        ).astype(BF16)
+        )
 
     def split(table):
         high = table.astype(BF16)
         return high, (table - high.astype(F32)).astype(BF16)
 
-    rise_wide = wide(falling * jnp.exp(-rate_c * middle))
-    fall_wide[...] = wide(weight_c * rising * jnp.exp(-rate_c * (span - 1.0 - middle)))
+    rise_wide, rise_wide_low = split(wide(falling * jnp.exp(-rate_c * middle)))
+    fall_wide[...] = wide(weight_c * rising * jnp.exp(-rate_c * (span - 1.0 - middle))).astype(BF16)
     from_middle_col = iota((span, lanes), 0).astype(F32) - middle
     fall_col = jnp.exp(-rate * from_middle_col)
     rise_col = jnp.exp(rate * from_middle_col)
-    tail = tall(rise_col * jnp.exp(-rate * (span - middle)))
-    decay_in = tall(fall_col * jnp.exp(-rate * middle))
+    tail, tail_low = split(tall(rise_col * jnp.exp(-rate * (span - middle))))
+    decay_in, decay_in_low = split(tall(fall_col * jnp.exp(-rate * middle)))
     rise_col = rise_col.astype(BF16)
 
     loads[0].wait()
@@ -196,7 +205,7 @@
 
     lax.fori_loop(0, spans, gate, 0, unroll=8)
 
-    state = dot(x_buf[...], tail)
+    state = dot(x_buf[...], tail) + dot(x_buf[...], tail_low)
     span_decay = jnp.exp(-rate * span)
     powers = jnp.exp(-rate * span * iota((spans, lanes), 0).astype(F32))
     run = jnp.zeros((width, lanes), F32)
@@ -216,9 +225,9 @@
             jnp.concatenate([fall_high[at], fall_high[at], fall_low[at]], axis=0),
             jnp.concatenate([rise_high[at], rise_low[at], rise_high[at]], axis=0),
         )
-        toep[g] = jnp.where(lower, toeplitz, 0.0).astype(BF16)
+        toep[g], toep_low[g] = split(jnp.where(lower, toeplitz, 0.0))
         at = slice(g * span, (g + 1) * span)
-        conv[:, at] = dot_nt(x_buf[:, at], toep[g])
+        conv[:, at] = dot_nt(x_buf[:, at], toep[g]) + dot_nt(x_buf[:, at], toep_low[g])
     for n in range(spans):
         power = jnp.broadcast_to(powers[n : n + 1], (width, lanes))
         fwd_pow[n * width : (n + 1) * width, :] = power
@@ -237,9 +246,10 @@
 
     enter = enter_buf[...] + fwd_pow[...] * entering(fwd_slots, True)
     enter_buf[...] = enter
-    conv[...] = conv[...] + dot(enter.astype(BF16), rise_wide)
-
-    send_to(range(nch * 3 // 4, nch))
+    enter, enter_low = split(enter)
+    conv[...] = (
+        conv[...] + dot(enter, rise_wide) + dot(enter_low, rise_wide) + dot(enter, rise_wide_low)
+    )
 
     loads[2].wait()
     skip_sum = jnp.zeros((channels, span), F32)
@@ -291,7 +301,7 @@
         at_batch = flip(lax.div(me, per_unit * batch_units), place)
         batch_rows = batch_units * unit_spans * width
         rows = pl.ds(pl.multiple_of(at_batch * batch_rows, batch_rows), batch_rows)
-        weighted = dot(g_buf[rows, :], decay_in)
+        weighted = dot(g_buf[rows, :], decay_in) + dot(g_buf[rows, :], decay_in_low)
         state = weighted * state_decay
         bwd_sum = bwd_sum + over_spans(state * fwd_pow[rows, :])
         if k == len(batches) - 1:
@@ -305,7 +315,7 @@
             cross = dot_tn(part, x_buf[rows, at])
             cross_buf[g] = cross if k == 0 else cross_buf[g] + cross
             if k < len(batches) - 1:
-                conv[rows, at] = conv[rows, at] + dot(part, toep[g])
+                conv[rows, at] = conv[rows, at] + dot(part, toep[g]) + dot(part, toep_low[g])
 
     filter_sum = jnp.sum(far_sum, axis=0, keepdims=True)
     for g in range(groups):
@@ -359,7 +369,7 @@
     groups = channels // width
     span = conv.shape[1] // groups
     spans = length // span
-    pieces = 4 if spans % 4 == 0 else 1
+    pieces = 8 if spans % 8 == 0 else 1
     piece_spans = spans // pieces
     copies = []
 
@@ -367,8 +377,9 @@
         copies.append(pltpu.make_async_copy(src, dst, sem.at[len(copies)]))
         copies[-1].start()
 
-    for p in range(pieces):
-        cols = pl.ds(p * piece_spans * span, piece_spans * span)
+    quarter = length // 4
+    for p in range(4):
+        cols = pl.ds(p * quarter, quarter)
         send(third.at[:, cols], out_third.at[:, cols])
     send(residue, out_residue)
     send(skip, out_skip)
@@ -424,6 +435,7 @@
             big_buf, pltpu.VMEM((nch, channels, length // nch), BF16),
             half_buf, half_buf,
             pltpu.VMEM((groups, span, span), F32),
+            pltpu.VMEM((groups, span, span), BF16),
             pltpu.VMEM((groups, span, span), BF16),
             state_buf, state_buf, state_buf,
             slots, slots,
@@ -456,7 +468,7 @@
         out_shape=(big, big, big, *small),
         in_specs=[vmem] * 8,
         out_specs=[whole] * 5,
-        scratch_shapes=[big_buf, big_buf, dma((14,))],
+        scratch_shapes=[big_buf, big_buf, dma((22,))],
         compiler_params=pltpu.CompilerParams(vmem_limit_bytes=16 * 1024 * 1024),
     )(*outs)
     return (*outs[:4], outs[4].reshape(channels))

time: 22.9 us -> 23.1 us (level)
  no operation moved by 1% of the time
where the time goes in v7:
time: 23.1 us; the launch traced here: 22.8 us
  Pallas kernels  22.1 us (96%)
  between operations  0.64 us (3%)
    pallas_call x1, Pallas kernels, on_device(): pl.pallas_call(functools.partial(kernel, dims), out_shape=(big, big, big,...  20.8 us
    pallas_call x1, Pallas kernels, on_device(): pl.pallas_call(functools.partial(finish, width), out_shape=(big, big, big...  1.33 us

profile of v7, /device:TPU:8, one launch (start us, length us, event | category | flops | bytes accessed | tf_op | source)
XLA Modules:
  0.0 22.8 jit_solution(454862465180375393)
XLA Ops:
  0.6 20.8 %shard_map.110 = (bf16[32,8192]{1,0:T(8,128)(2,1)S(1)}, bf16[32,8192]{1,0:T(8,128)(2,1)S(1)}, bf16[32,8192]{1,0:T(8,128)(2,1)S(1)}, f32[512,512]{1,0:T(8,128)S(1...) custom-call(bf16[32,8192]{1,0:T(8,128)(2,1)} %first_hbm.1, ...), custom_call_target="tpu_custom_call" | custom-call | flops 805306368 | bytes 3670016 | tf_op jit(solution)/shard_map/pallas_call | solution.py:423
  21.4 1.3 %shard_map.111 = (bf16[32,8192]{1,0:T(8,128)(2,1)}, bf16[32,8192]{1,0:T(8,128)(2,1)}, bf16[32,8192]{1,0:T(8,128)(2,1)}, f32[2,16]{1,0:T(2,128)}, f32[1,32]{1,0:T(1,128)}) custom-call(bf16[32,8192]{1,0:T(8,128)(2,1)S(1)} %get-tuple-element.18.first, bf16[32,8192]{1,0:T(8,128)(2,1)S(1)} %get-tuple-element.19.second, ...), custom_call_target="tpu_custom_call" | custom-call | tf_op jit(solution)/shard_map/pallas_call | solution.py:466
